TPU v7x, 32 devices: a whole 2x2x4 slice. The times are simulated.
32 devices in a mesh: section: 4 (over x, core), row: 8 (over z, y).
Axes of the slice: x: 2, y: 2, z: 4, core: 2. Of those that a mesh axis runs over, the one named last changes fastest.
Arguments:
- pair_in: bfloat16 [4, 256, 256, 128], P('section', 'row'), may hold values from -6 to 6
- upstream: bfloat16 [4, 256, 256, 128], P('section', 'row'), may hold values from -6 to 6
- chain_ids: int32 [256], replicated, may hold values from 0 to 2, never falling along the last dimension, each value on 1 to 192 neighbouring positions
- crop_mask: int32 [256], replicated, may hold values 0 or 1
- weight_in: bfloat16 [4, 2, 128, 640], P('section'), may hold values from -0.5 to 0.5
- weight_out: bfloat16 [4, 2, 128, 128], P('section'), may hold values from -0.5 to 0.5
- gain_in: float32 [4, 2, 128], P('section'), may hold values from 0.25 to 1.75
- bias_in: float32 [4, 2, 128], P('section'), may hold values from -3 to 3
- gain_out: float32 [4, 2, 128], P('section'), may hold values from 0.25 to 1.75
- bias_out: float32 [4, 2, 128], P('section'), may hold values from -3 to 3
Outputs:
- next_cotangent: bfloat16 [4, 256, 256, 128], P('section', 'row')
- grad_weight_in: float32 [4, 2, 128, 640], P('section')
- grad_weight_out: float32 [4, 2, 128, 128], P('section')
- grad_norm_in: float32 [4, 2, 2, 128], P('section')
- grad_norm_out: float32 [4, 2, 2, 128], P('section')
Inputs may be any that keep to these rules, and one draw needn't show every extreme that they name: `chain_ids`: chain numbers never fall along the residues; the longest chain holds 192 residues. `crop_mask`: 1 marks a residue present in the crop.
All inputs are finite; a program needn't handle non-finite values.
Results may differ from a plain program's by a relative error of at most 0.014.
Values may be sent and summed in bfloat16 or wider, within the bound.
A program may use at most 192 MiB of HBM per device.

v0:
```python
import jax
import jax.numpy as jnp
from jax import lax
from jax.sharding import PartitionSpec as P

epsilon = 1e-05


def passed_along(array, axis, by):
    length = lax.axis_size(axis)
    return lax.ppermute(array, axis, [(i, (i + by) % length) for i in range(length)])


def multiply(pattern, first_part, second):
    return jnp.einsum(pattern, first_part, second, preferred_element_type=jnp.float32)


def layer_inputs(pair_rows, pair_mask, weight_inner, gain_inner, bias_inner, hidden):
    values = pair_rows.astype(jnp.float32)
    centered = values - jnp.mean(values, axis=-1, keepdims=True)
    inverse_scale = lax.rsqrt(jnp.mean(centered * centered, axis=-1, keepdims=True) + epsilon)
    normal_in = centered * inverse_scale
    normed = (normal_in * gain_inner + bias_inner).astype(jnp.bfloat16)
    projected = multiply("rnc,cf->frn", normed, weight_inner[:, : 4 * hidden])
    gating = jax.nn.sigmoid(multiply("rnc,cf->rnf", normed, weight_inner[:, 4 * hidden :]))
    left_sigmoid = jax.nn.sigmoid(projected[:hidden])
    right_sigmoid = jax.nn.sigmoid(projected[2 * hidden : 3 * hidden])
    left_edges = (pair_mask * left_sigmoid * projected[hidden : 2 * hidden]).astype(jnp.bfloat16)
    right_edges = (pair_mask * right_sigmoid * projected[3 * hidden :]).astype(jnp.bfloat16)
    saved_in = (normal_in, inverse_scale, normed, projected, left_sigmoid, right_sigmoid, gating)
    return (left_edges, right_edges, saved_in)


def triangle_forward(left_edges, right_edges, outgoing):
    if outgoing:
        product = multiply("hik,hjk->hij", left_edges, right_edges)
    else:
        product = multiply("hki,hkj->hij", left_edges, right_edges)
    return product.astype(jnp.bfloat16)


def triangle_backward(grad_product, left_edges, right_edges, outgoing):
    if outgoing:
        grad_leftside = multiply("hij,hjk->hik", grad_product, right_edges)
        grad_rightside = multiply("hij,hik->hjk", grad_product, left_edges)
    else:
        grad_leftside = multiply("hij,hkj->hki", grad_product, right_edges)
        grad_rightside = multiply("hij,hki->hkj", grad_product, left_edges)
    return (grad_leftside.astype(jnp.bfloat16), grad_rightside.astype(jnp.bfloat16))


def layer_output(pair_rows, product, gating, gain_outer, bias_outer, weight_outer):
    values = product.astype(jnp.float32)
    centered = values - jnp.mean(values, axis=0, keepdims=True)
    inverse_scale = lax.rsqrt(jnp.mean(centered * centered, axis=0, keepdims=True) + epsilon)
    normal_out = centered * inverse_scale
    normed = (normal_out * gain_outer[:, None, None] + bias_outer[:, None, None]).astype(
        jnp.bfloat16
    )
    branch = multiply("hrn,hc->rnc", normed, weight_outer)
    updated = (pair_rows.astype(jnp.float32) + gating * branch).astype(jnp.bfloat16)
    return (updated, (normal_out, inverse_scale, normed, branch))


def output_backward(grad_pair, gating, saved_out, gain_outer, weight_outer):
    normal_out, inverse_scale, normed, branch = saved_out
    upstream_values = grad_pair.astype(jnp.float32)
    grad_branch = (upstream_values * gating).astype(jnp.bfloat16)
    grad_gate = (upstream_values * branch * gating * (1.0 - gating)).astype(jnp.bfloat16)
    grad_weight_out = multiply("hrn,rnc->hc", normed, grad_branch)
    grad_normed = multiply("rnc,hc->hrn", grad_branch, weight_outer)
    grad_gain = jnp.sum(grad_normed * normal_out, axis=(1, 2))
    grad_bias = jnp.sum(grad_normed, axis=(1, 2))
    scaled = grad_normed * gain_outer[:, None, None]
    grad_product = inverse_scale * (
        scaled
        - jnp.mean(scaled, axis=0, keepdims=True)
        - normal_out * jnp.mean(scaled * normal_out, axis=0, keepdims=True)
    )
    return (
        grad_product.astype(jnp.bfloat16),
        grad_gate,
        grad_weight_out,
        jnp.stack([grad_gain, grad_bias]),
    )


def input_backward(
    grad_leftside, grad_rightside, grad_gate, saved_in, pair_mask, weight_inner, gain_inner, hidden
):
    normal_in, inverse_scale, normed, projected, left_sigmoid, right_sigmoid, gating = saved_in
    left_values = grad_leftside.astype(jnp.float32) * pair_mask
    right_values = grad_rightside.astype(jnp.float32) * pair_mask
    grad_projected = jnp.concatenate(
        [
            left_values * projected[hidden : 2 * hidden] * left_sigmoid * (1.0 - left_sigmoid),
            left_values * left_sigmoid,
            right_values * projected[3 * hidden :] * right_sigmoid * (1.0 - right_sigmoid),
            right_values * right_sigmoid,
        ],
        axis=0,
    ).astype(jnp.bfloat16)
    grad_weight_in = jnp.concatenate(
        [
            multiply("rnc,frn->cf", normed, grad_projected),
            multiply("rnc,rnf->cf", normed, grad_gate),
        ],
        axis=1,
    )
    grad_normed = multiply("frn,cf->rnc", grad_projected, weight_inner[:, : 4 * hidden]) + multiply(
        "rnf,cf->rnc", grad_gate, weight_inner[:, 4 * hidden :]
    )
    grad_gain = jnp.sum(grad_normed * normal_in, axis=(0, 1))
    grad_bias = jnp.sum(grad_normed, axis=(0, 1))
    scaled = grad_normed * gain_inner
    grad_pair = inverse_scale * (
        scaled
        - jnp.mean(scaled, axis=-1, keepdims=True)
        - normal_in * jnp.mean(scaled * normal_in, axis=-1, keepdims=True)
    )
    return (grad_pair, grad_weight_in, jnp.stack([grad_gain, grad_bias]))


def per_device(
    pair_in,
    upstream,
    chain_ids,
    crop_mask,
    weight_in,
    weight_out,
    gain_in,
    bias_in,
    gain_out,
    bias_out,
):
    row_count = pair_in.shape[1]
    hidden = weight_out.shape[2]
    row_start = lax.axis_index("row") * row_count
    row_chain = lax.dynamic_slice_in_dim(chain_ids, row_start, row_count)
    row_crop = lax.dynamic_slice_in_dim(crop_mask, row_start, row_count)
    same_chain = row_chain[:, None] == chain_ids[None, :]
    pair_mask = jnp.where(same_chain, row_crop[:, None] * crop_mask[None, :], 0).astype(jnp.float32)
    pair_rows = pair_in[0]
    grad_top = upstream[0]

    def forward_update(source, direction, outgoing):
        left_edges, right_edges, saved_in = layer_inputs(
            source,
            pair_mask,
            weight_in[0, direction],
            gain_in[0, direction],
            bias_in[0, direction],
            hidden,
        )
        left_channels, right_channels = (
            lax.all_to_all(left_edges, "row", split_axis=0, concat_axis=1, tiled=True),
            lax.all_to_all(right_edges, "row", split_axis=0, concat_axis=1, tiled=True),
        )
        product = lax.all_to_all(
            triangle_forward(left_channels, right_channels, outgoing),
            "row",
            split_axis=1,
            concat_axis=0,
            tiled=True,
        )
        updated, saved_out = layer_output(
            source,
            product,
            saved_in[6],
            gain_out[0, direction],
            bias_out[0, direction],
            weight_out[0, direction],
        )
        return (updated, (left_channels, right_channels, saved_in, saved_out))

    def backward_update(grad_pair, stored, direction, outgoing):
        left_channels, right_channels, saved_in, saved_out = stored
        grad_product, grad_gate, grad_weight_out, grad_norm_out = output_backward(
            grad_pair, saved_in[6], saved_out, gain_out[0, direction], weight_out[0, direction]
        )
        grad_channels = lax.all_to_all(grad_product, "row", split_axis=0, concat_axis=1, tiled=True)
        left_grads, right_grads = triangle_backward(
            grad_channels, left_channels, right_channels, outgoing
        )
        grad_leftside, grad_rightside = (
            lax.all_to_all(left_grads, "row", split_axis=1, concat_axis=0, tiled=True),
            lax.all_to_all(right_grads, "row", split_axis=1, concat_axis=0, tiled=True),
        )
        branch_grad, grad_weight_in, grad_norm_in = input_backward(
            grad_leftside,
            grad_rightside,
            grad_gate,
            saved_in,
            pair_mask,
            weight_in[0, direction],
            gain_in[0, direction],
            hidden,
        )
        return (branch_grad, (grad_weight_in, grad_weight_out, grad_norm_in, grad_norm_out))

    middle, stored_outgoing = forward_update(pair_rows, 0, True)
    top_unused, stored_incoming = forward_update(middle, 1, False)
    grad_inner, sums_incoming = backward_update(grad_top, stored_incoming, 1, False)
    grad_middle = (grad_top.astype(jnp.float32) + grad_inner).astype(jnp.bfloat16)
    grad_outer, sums_outgoing = backward_update(grad_middle, stored_outgoing, 0, True)
    outer_rounded = lax.optimization_barrier(grad_outer.astype(jnp.bfloat16))
    grad_input = (grad_middle.astype(jnp.float32) + outer_rounded.astype(jnp.float32)).astype(
        jnp.bfloat16
    )
    passed_back = passed_along(grad_input, "section", -1)
    stacked = [jnp.stack([sums_outgoing[member], sums_incoming[member]]) for member in range(4)]
    totals = (
        lax.psum(stacked[0].astype(jnp.bfloat16), "row").astype(jnp.float32),
        lax.psum(stacked[1].astype(jnp.bfloat16), "row").astype(jnp.float32),
        lax.psum(stacked[2].astype(jnp.bfloat16), "row").astype(jnp.float32),
        lax.psum(stacked[3].astype(jnp.bfloat16), "row").astype(jnp.float32),
    )
    inverse_n = 1.0 / pair_rows.shape[1]
    return (
        passed_back[None],
        totals[0][None] * inverse_n,
        totals[1][None] * inverse_n,
        totals[2][None] * inverse_n,
        totals[3][None] * inverse_n,
    )


def solution(mesh):
    return jax.shard_map(
        per_device,
        mesh=mesh,
        in_specs=(
            P("section", "row", None, None),
            P("section", "row", None, None),
            P(),
            P(),
            P("section", None, None, None),
            P("section", None, None, None),
            P("section", None, None),
            P("section", None, None),
            P("section", None, None),
            P("section", None, None),
        ),
        out_specs=(
            P("section", "row", None, None),
            P("section", None, None, None),
            P("section", None, None, None),
            P("section", None, None, None),
            P("section", None, None, None),
        ),
        check_vma=False,
    )
```

profile of v0, /device:TPU:0, one launch (start us, length us, event | category | flops | bytes accessed | tf_op | source)
XLA Modules:
  0.0 907.4 jit_solution(7881545778491695648)
XLA Ops:
  17.0 5.3 multiply_convert_fusion.12
  24.0 4.5 copy.275
  28.6 7.3 all-to-all-start.1
  35.9 4.5 copy.273
  40.4 43.8 %all-to-all-done.1 = bf16[128,32,256]{2,1,0:T(8,128)(2,1)} async-done(((bf16[128,32,256]{2,1,0:T(8,128)(2,1)}), bf16[128,32,256]{2,1,0:T(8,128)(2,1)}, u32[]{:S(2)}, u32[]{:S(2)}) %all-to-all-start.1) | async-done | bytes 2097184 | tf_op jit(solution)/shard_map/all_to_all | solution.py:157
  84.2 4.4 all-to-all-start
  91.7 44.6 %all-to-all-done = bf16[128,32,256]{2,1,0:T(8,128)(2,1)} async-done(((bf16[128,32,256]{2,1,0:T(8,128)(2,1)}), bf16[128,32,256]{2,1,0:T(8,128)(2,1)}, u32[]{:S(2)}, u32[]{:S(2)}) %all-to-all-start) | async-done | bytes 2097184 | tf_op jit(solution)/shard_map/all_to_all | solution.py:156
  143.0 4.6 all-to-all-start.2
  148.4 46.9 %all-to-all-done.2 = bf16[16,256,256]{2,0,1:T(8,128)(2,1)} async-done(((bf16[16,256,256]{2,0,1:T(8,128)(2,1)}), bf16[16,256,256]{2,0,1:T(8,128)(2,1)}, u32[]{:S(2)}, u32[]{:S(2)}) %all-to-all-start.2) | async-done | bytes 2097184 | tf_op jit(solution)/shard_map/all_to_all | solution.py:159
  195.4 4.3 convert_bitcast_fusion.6
  213.0 5.1 multiply_convert_fusion.11
  219.4 4.6 copy.285
  224.0 4.4 all-to-all-start.3
  231.3 44.8 %all-to-all-done.3 = bf16[128,32,256]{2,1,0:T(8,128)(2,1)} async-done(((bf16[128,32,256]{2,1,0:T(8,128)(2,1)}), bf16[128,32,256]{2,1,0:T(8,128)(2,1)}, u32[]{:S(2)}, u32[]{:S(2)}) %all-to-all-start.3) | async-done | bytes 2097184 | tf_op jit(solution)/shard_map/all_to_all | solution.py:157
  276.2 4.7 all-to-all-start.4
  282.8 46.0 %all-to-all-done.4 = bf16[128,32,256]{2,1,0:T(8,128)(2,1)} async-done(((bf16[128,32,256]{2,1,0:T(8,128)(2,1)}), bf16[128,32,256]{2,1,0:T(8,128)(2,1)}, u32[]{:S(2)}, u32[]{:S(2)}) %all-to-all-start.4) | async-done | bytes 2097184 | tf_op jit(solution)/shard_map/all_to_all | solution.py:156
  335.1 4.3 all-to-all-start.5
  342.8 5.3 add_divide_fusion
  348.1 39.2 %all-to-all-done.5 = bf16[16,256,256]{2,0,1:T(8,128)(2,1)} async-done(((bf16[16,256,256]{2,0,1:T(8,128)(2,1)}), bf16[16,256,256]{2,0,1:T(8,128)(2,1)}, u32[]{:S(2)}, u32[]{:S(2)}) %all-to-all-start.5) | async-done | bytes 2097184 | tf_op jit(solution)/shard_map/all_to_all | solution.py:159
  393.1 5.3 copy.296
  398.4 7.5 fusion.53
  407.9 6.0 multiply_convert_fusion.9
  413.9 4.6 copy.297
  418.5 52.1 %all_to_all.162 = bf16[128,32,256]{2,1,0:T(8,128)(2,1)S(1)} all-to-all(bf16[128,32,256]{2,1,0:T(8,128)(2,1)} %copy.297), channel_id=1, replica_groups=mesh['section'=4,'row'=8] {'row'}, dimensions={0} | all-to-all | bytes 4194304 | tf_op jit(solution)/shard_map/all_to_all | solution.py:181
  474.7 4.5 all-to-all-start.7
  484.7 41.8 %all-to-all-done.7 = bf16[16,256,256]{2,0,1:T(8,128)(2,1)} async-done(((bf16[16,256,256]{2,0,1:T(8,128)(2,1)}), bf16[16,256,256]{2,0,1:T(8,128)(2,1)}, u32[]{:S(2)}, u32[]{:S(2)}) %all-to-all-start.7) | async-done | bytes 2097184 | tf_op jit(solution)/shard_map/all_to_all | solution.py:186
  526.5 4.4 all-to-all-start.8
  531.1 4.7 copy.317
  535.9 5.3 copy.318
  552.8 5.3 copy.302
  558.1 20.6 %all-to-all-done.8 = bf16[16,256,256]{2,0,1:T(8,128)(2,1)} async-done(((bf16[16,256,256]{2,0,1:T(8,128)(2,1)}), bf16[16,256,256]{2,0,1:T(8,128)(2,1)}, u32[]{:S(2)}, u32[]{:S(2)}) %all-to-all-start.8) | async-done | bytes 2097184 | tf_op jit(solution)/shard_map/all_to_all | solution.py:187
  583.8 5.3 copy.306
  589.1 10.0 %multiply_convert_fusion.8 = (bf16[128,32,256]{0,2,1:T(8,128)(2,1)S(1)}, bf16[128,32,256]{0,2,1:T(8,128)(2,1)S(1)}, bf16[128,32,256]{0,2,1:T(8,128)(2,1)S(1)}, bf16[128,32,256]{0,2,1:T(8,128)(2,1)S(1)}) fusion(f32[512,32,256]{0,2,1:T(8,128)} %copy-done.1, f32[128,32,256]{0,2,1:T(8,128)} %copy.302, f32[32,256]{1,0:T(8,128)S(1)} %select_convert_fusion, ...), kind=kLoop, calls=%fused_computation.95 | loop fusion | flops 23068672 | bytes 33587200 | tf_op jit(solution)/shard_map/convert.63
  611.7 5.5 fusion.52
  619.1 6.0 multiply_convert_fusion.4
  625.1 4.5 copy.319
  629.7 52.5 %all_to_all.163 = bf16[128,32,256]{2,1,0:T(8,128)(2,1)S(1)} all-to-all(bf16[128,32,256]{2,1,0:T(8,128)(2,1)} %copy.319), channel_id=1, replica_groups=mesh['section'=4,'row'=8] {'row'}, dimensions={0} | all-to-all | bytes 4194304 | tf_op jit(solution)/shard_map/all_to_all | solution.py:181
  686.3 4.3 all-to-all-start.10
  700.7 37.2 %all-to-all-done.10 = bf16[16,256,256]{2,0,1:T(8,128)(2,1)} async-done(((bf16[16,256,256]{2,0,1:T(8,128)(2,1)}), bf16[16,256,256]{2,0,1:T(8,128)(2,1)}, u32[]{:S(2)}, u32[]{:S(2)}) %all-to-all-start.10) | async-done | bytes 2097184 | tf_op jit(solution)/shard_map/all_to_all | solution.py:186
  737.9 4.4 all-to-all-start.11
  742.4 5.7 fusion.85
  751.7 5.7 fusion.86
  766.5 5.3 copy.324
  771.8 18.3 %all-to-all-done.11 = bf16[16,256,256]{2,0,1:T(8,128)(2,1)} async-done(((bf16[16,256,256]{2,0,1:T(8,128)(2,1)}), bf16[16,256,256]{2,0,1:T(8,128)(2,1)}, u32[]{:S(2)}, u32[]{:S(2)}) %all-to-all-start.11) | async-done | bytes 2097184 | tf_op jit(solution)/shard_map/all_to_all | solution.py:187
  795.2 5.3 copy.329
  800.6 10.1 %multiply_convert_fusion.3 = (bf16[128,32,256]{0,2,1:T(8,128)(2,1)S(1)}, bf16[128,32,256]{0,2,1:T(8,128)(2,1)S(1)}, bf16[128,32,256]{0,2,1:T(8,128)(2,1)S(1)}, bf16[128,32,256]{0,2,1:T(8,128)(2,1)S(1)}) fusion(f32[512,32,256]{0,2,1:T(8,128)} %copy-done, f32[128,32,256]{0,2,1:T(8,128)} %copy.324, f32[32,256]{1,0:T(8,128)S(1)} %select_convert_fusion, ...), kind=kLoop, calls=%fused_computation.87 | loop fusion | flops 23068672 | bytes 33587200 | tf_op jit(solution)/shard_map/convert.59
  822.0 20.7 %all-reduce = (bf16[2,2,128]{2,1,0:T(2,128)(2,1)S(1)}, bf16[2,2,128]{2,1,0:T(2,128)(2,1)S(1)}) all-reduce(bf16[2,2,128]{2,1,0:T(2,128)(2,1)S(1)} %pad_maximum_fusion.16, bf16[2,2,128]{2,1,0:T(2,128)(2,1)S(1)} %pad_maximum_fusion.17), channel_id=1, replica_groups=mesh['section'=4,'row'=8] {'row'}, use_global_device_ids=true, to_apply=%region_22.23 | all-reduce | flops 1024 | bytes 4096 | tf_op jit(solution)/shard_map/psum | solution.py:215
  843.8 49.0 %all-reduce.4.cloned.1.call-done = (bf16[2,128,640]{2,1,0:T(8,128)(2,1)}, bf16[2,128,128]{2,1,0:T(8,128)(2,1)}) async-done(((bf16[2,128,640]{2,1,0:T(8,128)(2,1)}, bf16[2,128,128]{2,1,0:T(8,128)(2,1)}), (bf16[2,128,640]{2,1,0:T(8,128)(2,1)}, bf16[2,128,128]{2,1,0:T(8,128)(2,1)})) %all-reduce.4.cloned.1.call-update) | async-done | bytes 393232 | tf_op jit(solution)/shard_map/psum | solution.py:213
  (230 shorter events, 151.0 us)
Async XLA Ops:
  9.9 195.4 %copy-start.41 = (bf16[1,1,128,640]{2,3,1,0:T(8,128)(2,1)}, bf16[1,1,128,640]{2,3,1,0:T(8,128)(2,1)S(1)}, u32[]{:S(2)}) copy-start(bf16[1,1,128,640]{2,3,1,0:T(8,128)(2,1)S(1)} %copy.382) | copy-start | bytes 491524
  9.9 4.5 copy-start.54
  9.9 4.5 copy-start.55
  9.9 4.5 copy-start.52
  9.9 4.5 copy-start.53
  13.3 192.0 %copy-start.2 = (bf16[1,32,256,128]{2,3,1,0:T(8,128)(2,1)}, bf16[1,32,256,128]{2,3,1,0:T(8,128)(2,1)S(1)}, u32[]{:S(2)}) copy-start(bf16[1,32,256,128]{2,3,1,0:T(8,128)(2,1)S(1)} %copy.268) | copy-start | bytes 6291460
  13.7 191.7 %copy-start.39 = (f32[32,256]{1,0:T(8,128)}, f32[32,256]{1,0:T(8,128)S(1)}, u32[]{:S(2)}) copy-start(f32[32,256]{1,0:T(8,128)S(1)} %broadcast_multiply_fusion.11) | copy-start | bytes 98308
  14.4 190.9 %copy-start.43 = (f32[32,256]{1,0:T(8,128)}, f32[32,256]{1,0:T(8,128)S(1)}, u32[]{:S(2)}) copy-start(f32[32,256]{1,0:T(8,128)S(1)} %add_rsqrt_fusion.3) | copy-start | bytes 98308
  14.4 190.9 %copy-start.46 = (f32[128]{0:T(128)}, f32[128]{0:T(128)S(1)}, u32[]{:S(2)}) copy-start(f32[128]{0:T(128)S(1)} %get-tuple-element.93) | copy-start | bytes 1540
  14.4 190.9 %copy-start.48 = (f32[128]{0:T(128)}, f32[128]{0:T(128)S(1)}, u32[]{:S(2)}) copy-start(f32[128]{0:T(128)S(1)} %get-tuple-element.87) | copy-start | bytes 1540
  17.0 7.0 copy-start
  28.6 55.6 %all-to-all-start.1 = ((bf16[128,32,256]{2,1,0:T(8,128)(2,1)}), bf16[128,32,256]{2,1,0:T(8,128)(2,1)}, u32[]{:S(2)}, u32[]{:S(2)}) async-start(bf16[128,32,256]{2,1,0:T(8,128)(2,1)} %copy.275), calls=%async_computation.1 | async-start | bytes 4194304 | tf_op jit(solution)/shard_map/all_to_all | solution.py:157
  84.2 52.2 %all-to-all-start = ((bf16[128,32,256]{2,1,0:T(8,128)(2,1)}), bf16[128,32,256]{2,1,0:T(8,128)(2,1)}, u32[]{:S(2)}, u32[]{:S(2)}) async-start(bf16[128,32,256]{2,1,0:T(8,128)(2,1)} %copy.273), calls=%async_computation | async-start | bytes 4194304 | tf_op jit(solution)/shard_map/all_to_all | solution.py:156
  136.4 3.3 copy-start.18
  140.5 7.1 copy-start.56
  140.5 7.1 copy-start.57
  143.0 52.4 %all-to-all-start.2 = ((bf16[16,256,256]{2,0,1:T(8,128)(2,1)}), bf16[16,256,256]{2,0,1:T(8,128)(2,1)}, u32[]{:S(2)}, u32[]{:S(2)}) async-start(bf16[16,256,256]{2,0,1:T(8,128)(2,1)} %copy.277), calls=%async_computation.2 | async-start | bytes 4194304 | tf_op jit(solution)/shard_map/all_to_all | solution.py:159
  205.4 3.8 copy-start.26
  213.0 6.4 copy-start.1
  224.0 52.2 %all-to-all-start.3 = ((bf16[128,32,256]{2,1,0:T(8,128)(2,1)}), bf16[128,32,256]{2,1,0:T(8,128)(2,1)}, u32[]{:S(2)}, u32[]{:S(2)}) async-start(bf16[128,32,256]{2,1,0:T(8,128)(2,1)} %copy.285), calls=%async_computation.3 | async-start | bytes 4194304 | tf_op jit(solution)/shard_map/all_to_all | solution.py:157
  276.2 52.6 %all-to-all-start.4 = ((bf16[128,32,256]{2,1,0:T(8,128)(2,1)}), bf16[128,32,256]{2,1,0:T(8,128)(2,1)}, u32[]{:S(2)}, u32[]{:S(2)}) async-start(bf16[128,32,256]{2,1,0:T(8,128)(2,1)} %copy.287), calls=%async_computation.4 | async-start | bytes 4194304 | tf_op jit(solution)/shard_map/all_to_all | solution.py:156
  282.7 49.9 %copy-start.21 = (bf16[16,8,32,256]{3,2,1,0:T(8,128)(2,1)}, bf16[16,8,32,256]{3,2,1,0:T(8,128)(2,1)S(1)}, u32[]{:S(2)}) copy-start(bf16[16,8,32,256]{3,2,1,0:T(8,128)(2,1)S(1)} %copy.286) | copy-start | bytes 6291460
  335.1 52.2 %all-to-all-start.5 = ((bf16[16,256,256]{2,0,1:T(8,128)(2,1)}), bf16[16,256,256]{2,0,1:T(8,128)(2,1)}, u32[]{:S(2)}, u32[]{:S(2)}) async-start(bf16[16,256,256]{2,0,1:T(8,128)(2,1)} %copy.290), calls=%async_computation.5 | async-start | bytes 4194304 | tf_op jit(solution)/shard_map/all_to_all | solution.py:159
  398.4 9.5 %copy-start.4 = (f32[128,32,256]{0,2,1:T(8,128)S(1)}, f32[128,32,256]{0,2,1:T(8,128)}, u32[]{:S(2)}) copy-start(f32[128,32,256]{0,2,1:T(8,128)} %copy.296) | copy-start | bytes 12582916
  418.5 52.3 %copy-start.22 = (bf16[16,8,32,256]{3,2,1,0:T(8,128)(2,1)S(1)}, bf16[16,8,32,256]{3,2,1,0:T(8,128)(2,1)}, u32[]{:S(2)}) copy-start(bf16[16,8,32,256]{3,2,1,0:T(8,128)(2,1)} %copy-done.21) | copy-start | bytes 6291460
  474.7 51.8 %all-to-all-start.7 = ((bf16[16,256,256]{2,0,1:T(8,128)(2,1)}), bf16[16,256,256]{2,0,1:T(8,128)(2,1)}, u32[]{:S(2)}, u32[]{:S(2)}) async-start(bf16[16,256,256]{2,0,1:T(8,128)(2,1)} %copy.299), calls=%async_computation.7 | async-start | bytes 4194304 | tf_op jit(solution)/shard_map/all_to_all | solution.py:186
  526.5 52.2 %all-to-all-start.8 = ((bf16[16,256,256]{2,0,1:T(8,128)(2,1)}), bf16[16,256,256]{2,0,1:T(8,128)(2,1)}, u32[]{:S(2)}, u32[]{:S(2)}) async-start(bf16[16,256,256]{2,0,1:T(8,128)(2,1)} %copy.303), calls=%async_computation.8 | async-start | bytes 4194304 | tf_op jit(solution)/shard_map/all_to_all | solution.py:187
  599.2 4.7 copy-start.31
  599.2 4.7 copy-start.33
  604.1 3.5 copy-start.27
  607.6 4.2 copy-start.5
  611.7 5.5 copy-start.13
  629.7 52.8 %copy-start.19 = (bf16[16,8,32,256]{3,2,1,0:T(8,128)(2,1)S(1)}, bf16[16,8,32,256]{3,2,1,0:T(8,128)(2,1)}, u32[]{:S(2)}) copy-start(bf16[16,8,32,256]{3,2,1,0:T(8,128)(2,1)} %copy.276) | copy-start | bytes 6291460
  686.3 51.6 %all-to-all-start.10 = ((bf16[16,256,256]{2,0,1:T(8,128)(2,1)}), bf16[16,256,256]{2,0,1:T(8,128)(2,1)}, u32[]{:S(2)}, u32[]{:S(2)}) async-start(bf16[16,256,256]{2,0,1:T(8,128)(2,1)} %copy.321), calls=%async_computation.10 | async-start | bytes 4194304 | tf_op jit(solution)/shard_map/all_to_all | solution.py:186
  693.9 3.3 copy-start.17
  693.9 3.5 copy-start.24
  698.2 44.2 %copy-start.51 = (f32[128]{0:T(128)S(1)}, f32[128]{0:T(128)}, u32[]{:S(2)}) copy-start(f32[128]{0:T(128)} %get-tuple-element.97) | copy-start | bytes 1540
  737.9 52.2 %all-to-all-start.11 = ((bf16[16,256,256]{2,0,1:T(8,128)(2,1)}), bf16[16,256,256]{2,0,1:T(8,128)(2,1)}, u32[]{:S(2)}, u32[]{:S(2)}) async-start(bf16[16,256,256]{2,0,1:T(8,128)(2,1)} %copy.326), calls=%async_computation.11 | async-start | bytes 4194304 | tf_op jit(solution)/shard_map/all_to_all | solution.py:187
  742.3 150.5 %all-reduce.4.cloned.1.call-start = ((), (), s32[]{:S(2)}) async-start(), calls=%async_computation.12 | async-start | bytes 786432 | tf_op jit(solution)/shard_map/psum | solution.py:213
  748.1 3.5 copy-start.14
  748.1 3.5 copy-start.50
  751.6 6.4 copy-start.12
  751.7 6.4 copy-start.32
  751.7 6.4 copy-start.34
  751.7 6.4 copy-start.36
  751.7 6.5 copy-start.38
  800.6 10.1 %copy-start.42 = (bf16[1,1,128,640]{2,3,1,0:T(8,128)(2,1)S(1)}, bf16[1,1,128,640]{2,3,1,0:T(8,128)(2,1)}, u32[]{:S(2)}) copy-start(bf16[1,1,128,640]{2,3,1,0:T(8,128)(2,1)} %copy-done.41) | copy-start | bytes 491524
  819.7 76.5 %collective-permute-start = (bf16[32,256,128]{1,2,0:T(8,128)(2,1)}, bf16[32,256,128]{1,2,0:T(8,128)(2,1)}, u32[]{:S(2)}, u32[]{:S(2)}) collective-permute-start(bf16[32,256,128]{1,2,0:T(8,128)(2,1)} %fusion.34), channel_id=1, source_target_pairs={{0,24},{8,0},{16,8},{24,16},{1,25},{9,1},{17,9},{25,17},{2,26},{10... | collective-permute-start | bytes 6291464 | tf_op jit(solution)/shard_map/ppermute | solution.py:11
  (22 other events, 45.3 us)
Sparse Core Ops, SparseCore 0:
  822.0 70.7 all-reduce.3
where the time goes:
time: 916 us; the launch traced here: 907 us
  waiting for transfers between devices  432 us (47%)
  local copies, waits for them, and re-layouts  138 us (15%)
  blocking collectives  125 us (14%)
  other arithmetic  81.4 us (9%)
  matrix products  67.3 us (7%)
  starting transfers between devices  47.3 us (5%)
  between operations  15.4 us (2%)
    all_to_all x2, blocking collectives, backward_update(): lax.all_to_all(grad_product, 'row', split_axis=0, concat_axis=1, tiled=True)  105 us
    all_to_all x2, waiting for transfers between devices, forward_update(): lax.all_to_all(left_edges, 'row', split_axis=0, concat_axis=1, tiled=True)  90.6 us
    all_to_all x2, waiting for transfers between devices, forward_update(): lax.all_to_all(right_edges, 'row', split_axis=0, concat_axis=1, tiled=True)  88.7 us
    all_to_all x2, waiting for transfers between devices, forward_update(): lax.all_to_all(triangle_forward(left_channels, right_channels, outgoing),...  86.2 us
    all_to_all x2, waiting for transfers between devices, backward_update(): lax.all_to_all(left_grads, 'row', split_axis=1, concat_axis=0, tiled=True)  79 us
    dot_general x24, matrix products, multiply(): jnp.einsum(pattern, first_part, second, preferred_element_type=jnp.float32)  67.3 us
    psum x1, waiting for transfers between devices, per_device(): lax.psum(stacked[0].astype(jnp.bfloat16), 'row').astype(jnp.float32)  49 us
    all_to_all x2, waiting for transfers between devices, backward_update(): lax.all_to_all(right_grads, 'row', split_axis=1, concat_axis=0, tiled=True)  38.9 us
  transfers between devices with their start and end apart: 12, of which 11 were waited for; matrix products, arithmetic and copies ran while one was open for 11% of the time, Pallas kernels for 0%

commit v1 on v0

--- a/solution.py
+++ b/solution.py
@@ -13,6 +13,59 @@
 
 def multiply(pattern, first_part, second):
     return jnp.einsum(pattern, first_part, second, preferred_element_type=jnp.float32)
+
+
+def fold(array):
+    quarter = array.shape[-1] // 4
+    half = array.shape[0] // 2
+    tail = array[..., 2 * quarter : 3 * quarter]
+    zeros = jnp.zeros_like(tail)
+    kept = array[..., : 2 * quarter] + jnp.concatenate([array[..., 3 * quarter :], zeros], axis=-1)
+    return jnp.concatenate([kept[:half], kept[half:], tail[:half], tail[half:]], axis=-1)
+
+
+def unfold(array, mask):
+    quarter = array.shape[-1] // 6
+
+    def one(kept, tail):
+        return jnp.concatenate([kept, tail, kept[..., :quarter]], axis=-1)
+
+    both = jnp.concatenate(
+        [
+            one(array[..., : 2 * quarter], array[..., 4 * quarter : 5 * quarter]),
+            one(array[..., 2 * quarter : 4 * quarter], array[..., 5 * quarter :]),
+        ],
+        axis=0,
+    )
+    if mask is None:
+        return both
+    return jnp.where(mask, both, jnp.zeros_like(both))
+
+
+def to_channels(array, mask):
+    moved = lax.all_to_all(fold(array), "row", split_axis=0, concat_axis=1, tiled=True)
+    return unfold(moved, mask)
+
+
+def to_rows(array, mask):
+    moved = lax.all_to_all(fold(array), "row", split_axis=1, concat_axis=0, tiled=True)
+    return unfold(moved, mask)
+
+
+def reduced(sums):
+    weights_in, weights_out, norm_in, norm_out = sums
+    norms = jnp.concatenate([norm_in, norm_out], axis=0)
+    columns = weights_out.shape[1]
+    norms = jnp.pad(norms, ((0, columns - norms.shape[0]), (0, 0))).T
+    flat = jnp.concatenate([weights_in, weights_out, norms], axis=1).astype(jnp.bfloat16)
+    width = lax.axis_size("row")
+    parts = flat.reshape(width, flat.shape[0] // width, flat.shape[1])
+    parts = lax.all_to_all(parts, "row", split_axis=0, concat_axis=0, tiled=True)
+    summed = jnp.sum(parts.astype(jnp.float32), axis=0).astype(jnp.bfloat16)
+    total = lax.all_gather(summed, "row", axis=0, tiled=True).astype(jnp.float32)
+    split = weights_in.shape[1]
+    norms = total[:, split + columns : split + columns + 4].T
+    return (total[:, :split], total[:, split : split + columns], norms[:2], norms[2:])
 
 
 def layer_inputs(pair_rows, pair_mask, weight_inner, gain_inner, bias_inner, hidden):
@@ -140,6 +193,10 @@
     row_crop = lax.dynamic_slice_in_dim(crop_mask, row_start, row_count)
     same_chain = row_chain[:, None] == chain_ids[None, :]
     pair_mask = jnp.where(same_chain, row_crop[:, None] * crop_mask[None, :], 0).astype(jnp.float32)
+    row_mask = pair_mask > 0
+    full_mask = (chain_ids[:, None] == chain_ids[None, :]) & (
+        (crop_mask[:, None] * crop_mask[None, :]) > 0
+    )
     pair_rows = pair_in[0]
     grad_top = upstream[0]
 
@@ -152,17 +209,9 @@
             bias_in[0, direction],
             hidden,
         )
-        left_channels, right_channels = (
-            lax.all_to_all(left_edges, "row", split_axis=0, concat_axis=1, tiled=True),
-            lax.all_to_all(right_edges, "row", split_axis=0, concat_axis=1, tiled=True),
-        )
-        product = lax.all_to_all(
-            triangle_forward(left_channels, right_channels, outgoing),
-            "row",
-            split_axis=1,
-            concat_axis=0,
-            tiled=True,
-        )
+        left_channels = to_channels(left_edges, full_mask)
+        right_channels = to_channels(right_edges, full_mask)
+        product = to_rows(triangle_forward(left_channels, right_channels, outgoing), row_mask)
         updated, saved_out = layer_output(
             source,
             product,
@@ -178,14 +227,15 @@
         grad_product, grad_gate, grad_weight_out, grad_norm_out = output_backward(
             grad_pair, saved_in[6], saved_out, gain_out[0, direction], weight_out[0, direction]
         )
-        grad_channels = lax.all_to_all(grad_product, "row", split_axis=0, concat_axis=1, tiled=True)
+        grad_product = jnp.where(row_mask, grad_product, jnp.zeros_like(grad_product))
+        grad_channels = to_channels(grad_product, full_mask)
         left_grads, right_grads = triangle_backward(
             grad_channels, left_channels, right_channels, outgoing
         )
-        grad_leftside, grad_rightside = (
-            lax.all_to_all(left_grads, "row", split_axis=1, concat_axis=0, tiled=True),
-            lax.all_to_all(right_grads, "row", split_axis=1, concat_axis=0, tiled=True),
-        )
+        left_grads = jnp.where(full_mask, left_grads, jnp.zeros_like(left_grads))
+        right_grads = jnp.where(full_mask, right_grads, jnp.zeros_like(right_grads))
+        grad_leftside = to_rows(left_grads, None)
+        grad_rightside = to_rows(right_grads, None)
         branch_grad, grad_weight_in, grad_norm_in = input_backward(
             grad_leftside,
             grad_rightside,
@@ -208,13 +258,11 @@
         jnp.bfloat16
     )
     passed_back = passed_along(grad_input, "section", -1)
-    stacked = [jnp.stack([sums_outgoing[member], sums_incoming[member]]) for member in range(4)]
-    totals = (
-        lax.psum(stacked[0].astype(jnp.bfloat16), "row").astype(jnp.float32),
-        lax.psum(stacked[1].astype(jnp.bfloat16), "row").astype(jnp.float32),
-        lax.psum(stacked[2].astype(jnp.bfloat16), "row").astype(jnp.float32),
-        lax.psum(stacked[3].astype(jnp.bfloat16), "row").astype(jnp.float32),
-    )
+    incoming_totals = reduced(sums_incoming)
+    outgoing_totals = reduced(sums_outgoing)
+    totals = [
+        jnp.stack([outgoing_totals[member], incoming_totals[member]]) for member in range(4)
+    ]
     inverse_n = 1.0 / pair_rows.shape[1]
     return (
         passed_back[None],

time: 916 us -> 857 us (0.936)
  waiting for transfers between devices: 432 us -> 304 us
  local copies, waits for them, and re-layouts: 138 us -> 210 us
  starting transfers between devices: 47.3 us -> 60.9 us
  between operations: 15.4 us -> 3.3 us
    unnamed x120 -> x290, local copies, waits for them, and re-layouts: 26.7 us -> 121 us
    convert_element_type x26 -> x0, local copies, waits for them, and re-layouts: 89.4 us -> none  [the longest x4 17.7 us: layer_output(): values = product.astype(jnp.float32)]
    all_to_all x10 -> x13, waiting for transfers between devices: 383 us -> 304 us  [the longest x6 149 us: to_rows(): lax.all_to_all(fold(array), 'row', split_axis=1, concat_axis=0, tiled=True)]
    all_gather x0 -> x2, blocking collectives: none -> 74.9 us  [reduced(): lax.all_gather(summed, 'row', axis=0, tiled=True).astype(jnp.float32)]
    all_to_all x2 -> x1, blocking collectives: 105 us -> 41 us  [to_channels(): lax.all_to_all(fold(array), 'row', split_axis=0, concat_axis=1, tiled=True)]
    psum x1 -> x0, waiting for transfers between devices: 49 us -> none  [per_device(): lax.psum(stacked[0].astype(jnp.bfloat16), 'row').astype(jnp.float32)]
    concatenate x0 -> x12, local copies, waits for them, and re-layouts: none -> 35 us  [fold(): jnp.concatenate([kept[:half], kept[half:], tail[:half], tail[half:]], axi...]
    slice x1 -> x60, local copies, waits for them, and re-layouts: 0.52 us -> 33.5 us  [the longest x12 16.9 us: unfold(): array[..., 4 * quarter:5 * quarter]]
  transfers between devices with their start and end apart: 12 -> 14, of which waited for: 11 -> 11; matrix products, arithmetic and copies ran while one was open for 11% -> 12% of each run, Pallas kernels for 0% -> 0%
where the time goes in v1:
time: 857 us; the launch traced here: 846 us
  waiting for transfers between devices  304 us (35%)
  local copies, waits for them, and re-layouts  210 us (25%)
  blocking collectives  116 us (14%)
  other arithmetic  82.3 us (10%)
  matrix products  70.1 us (8%)
  starting transfers between devices  60.9 us (7%)
    all_to_all x6, waiting for transfers between devices, to_rows(): lax.all_to_all(fold(array), 'row', split_axis=1, concat_axis=0, tiled=True)  149 us
    all_to_all x5, waiting for transfers between devices, to_channels(): lax.all_to_all(fold(array), 'row', split_axis=0, concat_axis=1, tiled=True)  146 us
    unnamed x290, local copies, waits for them, and re-layouts  121 us
    all_gather x2, blocking collectives, reduced(): lax.all_gather(summed, 'row', axis=0, tiled=True).astype(jnp.float32)  74.9 us
    dot_general x24, matrix products, multiply(): jnp.einsum(pattern, first_part, second, preferred_element_type=jnp.float32)  70.1 us
    all_to_all x1, blocking collectives, to_channels(): lax.all_to_all(fold(array), 'row', split_axis=0, concat_axis=1, tiled=True)  41 us
    concatenate x12, local copies, waits for them, and re-layouts, fold(): jnp.concatenate([kept[:half], kept[half:], tail[:half], tail[half:]], axi...  35 us
    all_to_all x6, starting transfers between devices, to_rows(): lax.all_to_all(fold(array), 'row', split_axis=1, concat_axis=0, tiled=True)  28.4 us
  transfers between devices with their start and end apart: 14, of which 11 were waited for; matrix products, arithmetic and copies ran while one was open for 12% of the time, Pallas kernels for 0%

profile of v1, /device:TPU:0, one launch (start us, length us, event | category | flops | bytes accessed | tf_op | source)
XLA Modules:
  0.0 846.0 jit_solution(3344272591239111677)
XLA Ops:
  3.4 3.3 copy.460
  10.5 5.1 multiply_convert_fusion.11
  20.1 4.8 copy.473
  25.0 7.3 all-to-all-start.1
  38.8 4.8 copy.465
  43.7 25.7 %all-to-all-done.1 = bf16[64,32,384]{2,1,0:T(8,128)(2,1)} async-done(((bf16[64,32,384]{2,1,0:T(8,128)(2,1)}), bf16[64,32,384]{2,1,0:T(8,128)(2,1)}, u32[]{:S(2)}, u32[]{:S(2)}) %all-to-all-start.1) | async-done | bytes 1572896 | tf_op jit(solution)/shard_map/all_to_all | solution.py:46
  69.3 4.5 all-to-all-start
  77.7 32.8 %all-to-all-done = bf16[64,32,384]{2,1,0:T(8,128)(2,1)} async-done(((bf16[64,32,384]{2,1,0:T(8,128)(2,1)}), bf16[64,32,384]{2,1,0:T(8,128)(2,1)}, u32[]{:S(2)}, u32[]{:S(2)}) %all-to-all-start) | async-done | bytes 1572896 | tf_op jit(solution)/shard_map/all_to_all | solution.py:46
  141.0 4.6 all-to-all-start.2
  146.2 36.0 %all-to-all-done.2 = bf16[8,256,384]{2,0,1:T(8,128)(2,1)} async-done(((bf16[8,256,384]{2,0,1:T(8,128)(2,1)}), bf16[8,256,384]{2,0,1:T(8,128)(2,1)}, u32[]{:S(2)}, u32[]{:S(2)}) %all-to-all-start.2) | async-done | bytes 1572896 | tf_op jit(solution)/shard_map/all_to_all | solution.py:51
  188.9 4.6 convert_reduce_fusion.1
  197.4 5.0 multiply_convert_fusion.9
  205.7 3.3 copy.496
  208.9 4.9 all-to-all-start.4
  216.7 3.2 copy.488
  219.9 30.6 %all-to-all-done.4 = bf16[64,32,384]{2,1,0:T(8,128)(2,1)} async-done(((bf16[64,32,384]{2,1,0:T(8,128)(2,1)}), bf16[64,32,384]{2,1,0:T(8,128)(2,1)}, u32[]{:S(2)}, u32[]{:S(2)}) %all-to-all-start.4) | async-done | bytes 1572896 | tf_op jit(solution)/shard_map/all_to_all | solution.py:46
  250.4 3.6 all-to-all-start.3
  257.6 33.7 %all-to-all-done.3 = bf16[64,32,384]{2,1,0:T(8,128)(2,1)S(1)} async-done(((bf16[64,32,384]{2,1,0:T(8,128)(2,1)}), bf16[64,32,384]{2,1,0:T(8,128)(2,1)S(1)}, u32[]{:S(2)}, u32[]{:S(2)}) %all-to-all-start.3) | async-done | bytes 1572896 | tf_op jit(solution)/shard_map/all_to_all | solution.py:46
  310.6 4.6 all-to-all-start.5
  315.2 4.1 copy.459
  319.3 3.8 add_divide_fusion
  323.1 28.7 %all-to-all-done.5 = bf16[8,256,384]{2,0,1:T(8,128)(2,1)} async-done(((bf16[8,256,384]{2,0,1:T(8,128)(2,1)}), bf16[8,256,384]{2,0,1:T(8,128)(2,1)}, u32[]{:S(2)}, u32[]{:S(2)}) %all-to-all-start.5) | async-done | bytes 1572896 | tf_op jit(solution)/shard_map/all_to_all | solution.py:51
  364.5 41.0 %all_to_all.226 = bf16[64,32,384]{2,1,0:T(8,128)(2,1)S(1)} all-to-all(bf16[64,32,384]{2,1,0:T(8,128)(2,1)S(1)} %copy.511), channel_id=1, replica_groups=mesh['section'=4,'row'=8] {'row'}, dimensions={0} | all-to-all | bytes 3145728 | tf_op jit(solution)/shard_map/all_to_all | solution.py:46
  423.6 4.3 all-to-all-start.8
  435.4 28.7 %all-to-all-done.8 = bf16[8,256,384]{2,0,1:T(8,128)(2,1)} async-done(((bf16[8,256,384]{2,0,1:T(8,128)(2,1)}), bf16[8,256,384]{2,0,1:T(8,128)(2,1)}, u32[]{:S(2)}, u32[]{:S(2)}) %all-to-all-start.8) | async-done | bytes 1572896 | tf_op jit(solution)/shard_map/all_to_all | solution.py:51
  464.1 4.3 all-to-all-start.7
  468.4 6.0 fusion.68
  478.9 26.0 %all-to-all-done.7 = bf16[8,256,384]{2,0,1:T(8,128)(2,1)} async-done(((bf16[8,256,384]{2,0,1:T(8,128)(2,1)}), bf16[8,256,384]{2,0,1:T(8,128)(2,1)}, u32[]{:S(2)}, u32[]{:S(2)}) %all-to-all-start.7) | async-done | bytes 1572896 | tf_op jit(solution)/shard_map/all_to_all | solution.py:51
  537.9 6.6 multiply_convert_fusion.5
  544.7 7.4 multiply_convert_fusion.7
  561.0 4.2 fusion.63
  573.8 4.7 all-to-all-start.9
  581.1 3.3 fusion.103
  586.6 4.8 fusion.98
  592.1 23.0 %all-to-all-done.9 = bf16[64,32,384]{2,1,0:T(8,128)(2,1)} async-done(((bf16[64,32,384]{2,1,0:T(8,128)(2,1)}), bf16[64,32,384]{2,1,0:T(8,128)(2,1)}, u32[]{:S(2)}, u32[]{:S(2)}) %all-to-all-start.9) | async-done | bytes 1572896 | tf_op jit(solution)/shard_map/all_to_all | solution.py:46
  615.1 3.6 all-to-all-start.13
  629.2 6.0 all-to-all-start.11
  642.3 29.7 %all-to-all-done.11 = bf16[8,256,384]{2,0,1:T(8,128)(2,1)} async-done(((bf16[8,256,384]{2,0,1:T(8,128)(2,1)}), bf16[8,256,384]{2,0,1:T(8,128)(2,1)}, u32[]{:S(2)}, u32[]{:S(2)}) %all-to-all-start.11) | async-done | bytes 1572896 | tf_op jit(solution)/shard_map/all_to_all | solution.py:51
  672.0 4.7 all-to-all-start.10
  681.6 3.7 fusion.105
  685.3 4.1 fusion.102
  689.5 44.1 %all_gather.7 = bf16[128,896]{1,0:T(8,128)(2,1)S(1)} all-gather(bf16[16,896]{1,0:T(8,128)(2,1)S(1)} %reduce_sum.265), channel_id=1, replica_groups=mesh['section'=4,'row'=8] {'row'}, dimensions={0}, use_global_device_ids=true | all-gather | bytes 258048 | tf_op jit(solution)/shard_map/all_gather | solution.py:65
  772.3 6.7 multiply_convert_fusion.1
  779.1 5.8 multiply_convert_fusion.3
  795.0 3.8 all-to-all-start.12
  798.8 9.0 %all-to-all-done.12 = bf16[8,16,896]{2,1,0:T(8,128)(2,1)S(1)} async-done(((bf16[8,16,896]{2,1,0:T(8,128)(2,1)}), bf16[8,16,896]{2,1,0:T(8,128)(2,1)S(1)}, u32[]{:S(2)}, u32[]{:S(2)}) %all-to-all-start.12) | async-done | bytes 229408 | tf_op jit(solution)/shard_map/all_to_all | solution.py:63
  807.9 30.8 %all_gather.6 = bf16[128,896]{1,0:T(8,128)(2,1)S(1)} all-gather(bf16[16,896]{1,0:T(8,128)(2,1)S(1)} %reduce_sum.260), channel_id=1, replica_groups=mesh['section'=4,'row'=8] {'row'}, dimensions={0}, use_global_device_ids=true | all-gather | bytes 258048 | tf_op jit(solution)/shard_map/all_gather | solution.py:65
  841.8 4.1 copy.592
  (476 shorter events, 263.4 us)
Async XLA Ops:
  6.7 182.1 %copy-start.2 = (bf16[1,32,256,128]{2,3,1,0:T(8,128)(2,1)}, bf16[1,32,256,128]{2,3,1,0:T(8,128)(2,1)S(1)}, u32[]{:S(2)}) copy-start(bf16[1,32,256,128]{2,3,1,0:T(8,128)(2,1)S(1)} %copy.460) | copy-start | bytes 6291460
  7.1 181.7 %copy-start.50 = (f32[32,256]{1,0:T(8,128)}, f32[32,256]{1,0:T(8,128)S(1)}, u32[]{:S(2)}) copy-start(f32[32,256]{1,0:T(8,128)S(1)} %broadcast_multiply_fusion.11) | copy-start | bytes 98308
  7.9 181.0 %copy-start.54 = (f32[32,256]{1,0:T(8,128)}, f32[32,256]{1,0:T(8,128)S(1)}, u32[]{:S(2)}) copy-start(f32[32,256]{1,0:T(8,128)S(1)} %add_rsqrt_fusion.3) | copy-start | bytes 98308
  7.9 180.9 %copy-start.91 = (f32[128]{0:T(128)}, f32[128]{0:T(128)S(1)}, u32[]{:S(2)}) copy-start(f32[128]{0:T(128)S(1)} %get-tuple-element.203) | copy-start | bytes 1540
  7.9 180.9 %copy-start.97 = (f32[128]{0:T(128)}, f32[128]{0:T(128)S(1)}, u32[]{:S(2)}) copy-start(f32[128]{0:T(128)S(1)} %get-tuple-element.197) | copy-start | bytes 1540
  7.9 311.3 %copy-start.101 = (f32[128]{0:T(128)}, f32[128]{0:T(128)S(1)}, u32[]{:S(2)}) copy-start(f32[128]{0:T(128)S(1)} %get-tuple-element.196) | copy-start | bytes 1540
  25.0 44.4 %all-to-all-start.1 = ((bf16[64,32,384]{2,1,0:T(8,128)(2,1)}), bf16[64,32,384]{2,1,0:T(8,128)(2,1)}, u32[]{:S(2)}, u32[]{:S(2)}) async-start(bf16[64,32,384]{2,1,0:T(8,128)(2,1)} %copy.473), calls=%async_computation.1 | async-start | bytes 3145728 | tf_op jit(solution)/shard_map/all_to_all | solution.py:46
  69.3 41.1 %all-to-all-start = ((bf16[64,32,384]{2,1,0:T(8,128)(2,1)}), bf16[64,32,384]{2,1,0:T(8,128)(2,1)}, u32[]{:S(2)}, u32[]{:S(2)}) async-start(bf16[64,32,384]{2,1,0:T(8,128)(2,1)} %copy.465), calls=%async_computation | async-start | bytes 3145728 | tf_op jit(solution)/shard_map/all_to_all | solution.py:46
  74.0 59.5 %copy-start.87 = (pred[256,256]{0,1:T(8,128)(4,1)}, pred[256,256]{0,1:T(8,128)(4,1)S(1)}, u32[]{:S(2)}) copy-start(pred[256,256]{0,1:T(8,128)(4,1)S(1)} %fusion.108) | copy-start | bytes 196612
  116.1 10.9 %copy-start.39 = (bf16[8,256,128]{2,1,0:T(8,128)(2,1)S(1)}, bf16[8,256,128]{2,1,0:T(8,128)(2,1)}, u32[]{:S(2)}) copy-start(bf16[8,256,128]{2,1,0:T(8,128)(2,1)} %get-tuple-element.149) | copy-start | bytes 1572868
  117.2 15.4 %copy-start.41 = (bf16[8,256,64]{2,1,0:T(8,128)(2,1)S(1)}, bf16[8,256,64]{2,1,0:T(8,128)(2,1)}, u32[]{:S(2)}) copy-start(bf16[8,256,64]{2,1,0:T(8,128)(2,1)} %get-tuple-element.153) | copy-start | bytes 786436
  136.8 8.8 %copy-start.111 = (f32[1,2,128]{2,1,0:T(2,128)S(1)}, f32[1,2,128]{2,1,0:T(2,128)}, u32[]{:S(2)}) copy-start(f32[1,2,128]{2,1,0:T(2,128)} %param.19) | copy-start | bytes 3076
  136.8 8.8 %copy-start.112 = (f32[1,2,128]{2,1,0:T(2,128)S(1)}, f32[1,2,128]{2,1,0:T(2,128)}, u32[]{:S(2)}) copy-start(f32[1,2,128]{2,1,0:T(2,128)} %param.18) | copy-start | bytes 3076
  136.8 9.3 %copy-start.106 = (s32[32]{0:T(128)S(1)}, s32[32]{0:T(128)}, u32[]{:S(2)}) copy-start(s32[32]{0:T(128)} %copy-done.105) | copy-start | bytes 388
  141.0 41.2 %all-to-all-start.2 = ((bf16[8,256,384]{2,0,1:T(8,128)(2,1)}), bf16[8,256,384]{2,0,1:T(8,128)(2,1)}, u32[]{:S(2)}, u32[]{:S(2)}) async-start(bf16[8,256,384]{2,0,1:T(8,128)(2,1)} %copy.483), calls=%async_computation.2 | async-start | bytes 3145728 | tf_op jit(solution)/shard_map/all_to_all | solution.py:51
  146.1 41.1 %copy-start.93 = (f32[128]{0:T(128)}, f32[128]{0:T(128)S(1)}, u32[]{:S(2)}) copy-start(f32[128]{0:T(128)S(1)} %get-tuple-element.205) | copy-start | bytes 1540
  146.1 41.1 %copy-start.99 = (f32[128]{0:T(128)}, f32[128]{0:T(128)S(1)}, u32[]{:S(2)}) copy-start(f32[128]{0:T(128)S(1)} %get-tuple-element.191) | copy-start | bytes 1540
  146.1 322.3 %copy-start.95 = (f32[128]{0:T(128)}, f32[128]{0:T(128)S(1)}, u32[]{:S(2)}) copy-start(f32[128]{0:T(128)S(1)} %get-tuple-element.206) | copy-start | bytes 1540
  208.9 41.5 %all-to-all-start.4 = ((bf16[64,32,384]{2,1,0:T(8,128)(2,1)}), bf16[64,32,384]{2,1,0:T(8,128)(2,1)}, u32[]{:S(2)}, u32[]{:S(2)}) async-start(bf16[64,32,384]{2,1,0:T(8,128)(2,1)} %copy.496), calls=%async_computation.4 | async-start | bytes 3145728 | tf_op jit(solution)/shard_map/all_to_all | solution.py:46
  250.4 40.8 %all-to-all-start.3 = ((bf16[64,32,384]{2,1,0:T(8,128)(2,1)}), bf16[64,32,384]{2,1,0:T(8,128)(2,1)S(1)}, u32[]{:S(2)}, u32[]{:S(2)}) async-start(bf16[64,32,384]{2,1,0:T(8,128)(2,1)} %copy.488), calls=%async_computation.3 | async-start | bytes 3145728 | tf_op jit(solution)/shard_map/all_to_all | solution.py:46
  291.7 7.7 copy-start.40
  294.5 10.9 %copy-start.42 = (bf16[8,256,64]{2,1,0:T(8,128)(2,1)S(1)}, bf16[8,256,64]{2,1,0:T(8,128)(2,1)}, u32[]{:S(2)}) copy-start(bf16[8,256,64]{2,1,0:T(8,128)(2,1)} %get-tuple-element.135) | copy-start | bytes 786436
  295.5 9.0 %copy-start.43 = (bf16[8,256,64]{2,1,0:T(8,128)(2,1)S(1)}, bf16[8,256,64]{2,1,0:T(8,128)(2,1)}, u32[]{:S(2)}) copy-start(bf16[8,256,64]{2,1,0:T(8,128)(2,1)} %get-tuple-element.134) | copy-start | bytes 786436
  295.5 10.1 %copy-start.88 = (pred[256,256]{0,1:T(8,128)(4,1)S(1)}, pred[256,256]{0,1:T(8,128)(4,1)}, u32[]{:S(2)}) copy-start(pred[256,256]{0,1:T(8,128)(4,1)} %copy-done.87) | copy-start | bytes 196612
  310.6 8.7 %copy-start.11 = (bf16[32,256,128]{1,2,0:T(8,128)(2,1)S(1)}, bf16[32,256,128]{1,2,0:T(8,128)(2,1)}, u32[]{:S(2)}) copy-start(bf16[32,256,128]{1,2,0:T(8,128)(2,1)} %copy-done.10) | copy-start | bytes 6291460
  310.6 41.2 %all-to-all-start.5 = ((bf16[8,256,384]{2,0,1:T(8,128)(2,1)}), bf16[8,256,384]{2,0,1:T(8,128)(2,1)}, u32[]{:S(2)}, u32[]{:S(2)}) async-start(bf16[8,256,384]{2,0,1:T(8,128)(2,1)} %copy.505), calls=%async_computation.5 | async-start | bytes 3145728 | tf_op jit(solution)/shard_map/all_to_all | solution.py:51
  408.7 7.6 copy-start.68
  411.0 7.9 copy-start.79
  419.3 8.6 %copy-start.64 = (bf16[8,256,128]{1,2,0:T(8,128)(2,1)S(1)}, bf16[8,256,128]{1,2,0:T(8,128)(2,1)}, u32[]{:S(2)}) copy-start(bf16[8,256,128]{1,2,0:T(8,128)(2,1)} %copy-done.63) | copy-start | bytes 1572868
  423.6 40.5 %all-to-all-start.8 = ((bf16[8,256,384]{2,0,1:T(8,128)(2,1)}), bf16[8,256,384]{2,0,1:T(8,128)(2,1)}, u32[]{:S(2)}, u32[]{:S(2)}) async-start(bf16[8,256,384]{2,0,1:T(8,128)(2,1)} %copy.531), calls=%async_computation.8 | async-start | bytes 3145728 | tf_op jit(solution)/shard_map/all_to_all | solution.py:51
  431.2 37.2 %copy-start.83 = (bf16[1,2,128,128]{3,2,1,0:T(8,128)(2,1)S(1)}, bf16[1,2,128,128]{3,2,1,0:T(8,128)(2,1)}, u32[]{:S(2)}) copy-start(bf16[1,2,128,128]{3,2,1,0:T(8,128)(2,1)} %param.15) | copy-start | bytes 196612
  431.2 37.2 %copy-start.107 = (f32[128]{0:T(128)S(1)}, f32[128]{0:T(128)}, u32[]{:S(2)}) copy-start(f32[128]{0:T(128)} %get-tuple-element.190) | copy-start | bytes 1540
  464.1 40.8 %all-to-all-start.7 = ((bf16[8,256,384]{2,0,1:T(8,128)(2,1)}), bf16[8,256,384]{2,0,1:T(8,128)(2,1)}, u32[]{:S(2)}, u32[]{:S(2)}) async-start(bf16[8,256,384]{2,0,1:T(8,128)(2,1)} %copy.521), calls=%async_computation.7 | async-start | bytes 3145728 | tf_op jit(solution)/shard_map/all_to_all | solution.py:51
  544.6 7.4 copy-start.44
  573.8 41.3 %all-to-all-start.9 = ((bf16[64,32,384]{2,1,0:T(8,128)(2,1)}), bf16[64,32,384]{2,1,0:T(8,128)(2,1)}, u32[]{:S(2)}, u32[]{:S(2)}) async-start(bf16[64,32,384]{2,1,0:T(8,128)(2,1)} %copy.547), calls=%async_computation.9 | async-start | bytes 3145728 | tf_op jit(solution)/shard_map/all_to_all | solution.py:46
  615.1 14.1 %all-to-all-start.13 = ((bf16[8,16,896]{2,1,0:T(8,128)(2,1)}), bf16[8,16,896]{2,1,0:T(8,128)(2,1)S(1)}, u32[]{:S(2)}, u32[]{:S(2)}) async-start(bf16[8,16,896]{2,1,0:T(8,128)(2,1)} %pad_maximum_fusion.23), calls=%async_computation.13 | async-start | bytes 458752 | tf_op jit(solution)/shard_map/all_to_all | solution.py:63
  627.0 8.2 copy-start.60
  627.0 8.2 copy-start.61
  627.2 8.1 copy-start.69
  629.2 42.7 %all-to-all-start.11 = ((bf16[8,256,384]{2,0,1:T(8,128)(2,1)}), bf16[8,256,384]{2,0,1:T(8,128)(2,1)}, u32[]{:S(2)}, u32[]{:S(2)}) async-start(bf16[8,256,384]{2,0,1:T(8,128)(2,1)} %copy.566), calls=%async_computation.11 | async-start | bytes 3145728 | tf_op jit(solution)/shard_map/all_to_all | solution.py:51
  638.1 38.6 %copy-start.3 = (bf16[1,32,256,128]{2,3,1,0:T(8,128)(2,1)S(1)}, bf16[1,32,256,128]{2,3,1,0:T(8,128)(2,1)}, u32[]{:S(2)}) copy-start(bf16[1,32,256,128]{2,3,1,0:T(8,128)(2,1)} %copy-done.2) | copy-start | bytes 6291460
  638.1 38.6 %copy-start.51 = (f32[32,256]{1,0:T(8,128)S(1)}, f32[32,256]{1,0:T(8,128)}, u32[]{:S(2)}) copy-start(f32[32,256]{1,0:T(8,128)} %copy-done.50) | copy-start | bytes 98308
  638.1 38.6 %copy-start.55 = (f32[32,256]{1,0:T(8,128)S(1)}, f32[32,256]{1,0:T(8,128)}, u32[]{:S(2)}) copy-start(f32[32,256]{1,0:T(8,128)} %copy-done.54) | copy-start | bytes 98308
  638.1 38.6 %copy-start.92 = (f32[128]{0:T(128)S(1)}, f32[128]{0:T(128)}, u32[]{:S(2)}) copy-start(f32[128]{0:T(128)} %copy-done.91) | copy-start | bytes 1540
  638.1 38.6 %copy-start.98 = (f32[128]{0:T(128)S(1)}, f32[128]{0:T(128)}, u32[]{:S(2)}) copy-start(f32[128]{0:T(128)} %copy-done.97) | copy-start | bytes 1540
  672.0 67.1 %all-to-all-start.10 = ((bf16[8,256,384]{2,0,1:T(8,128)(2,1)}), bf16[8,256,384]{2,0,1:T(8,128)(2,1)}, u32[]{:S(2)}, u32[]{:S(2)}) async-start(bf16[8,256,384]{2,0,1:T(8,128)(2,1)} %copy.556), calls=%async_computation.10 | async-start | bytes 3145728 | tf_op jit(solution)/shard_map/all_to_all | solution.py:51
  794.1 47.7 %collective-permute-start = (bf16[32,256,128]{1,2,0:T(8,128)(2,1)S(1)}, bf16[32,256,128]{1,2,0:T(8,128)(2,1)}, u32[]{:S(2)}, u32[]{:S(2)}) collective-permute-start(bf16[32,256,128]{1,2,0:T(8,128)(2,1)S(1)} %fusion.64), channel_id=1, source_target_pairs={{0,24},{8,0},{16,8},{24,16},{1,25},{9,1},{17,9},{25,17},{2,26},{10... | collective-permute-start | bytes 6291464 | tf_op jit(solution)/shard_map/ppermute | solution.py:11
  795.0 12.9 %all-to-all-start.12 = ((bf16[8,16,896]{2,1,0:T(8,128)(2,1)}), bf16[8,16,896]{2,1,0:T(8,128)(2,1)S(1)}, u32[]{:S(2)}, u32[]{:S(2)}) async-start(bf16[8,16,896]{2,1,0:T(8,128)(2,1)} %pad_maximum_fusion.22), calls=%async_computation.12 | async-start | bytes 458752 | tf_op jit(solution)/shard_map/all_to_all | solution.py:63
  (79 other events, 335.7 us)

commit v2 on v0

--- a/solution.py
+++ b/solution.py
@@ -1,6 +1,7 @@
 import jax
 import jax.numpy as jnp
 from jax import lax
+from jax.experimental import pallas as pl
 from jax.sharding import PartitionSpec as P
 
 epsilon = 1e-05
@@ -13,6 +14,148 @@
 
 def multiply(pattern, first_part, second):
     return jnp.einsum(pattern, first_part, second, preferred_element_type=jnp.float32)
+
+
+def low_lanes(array):
+    return lax.broadcasted_iota(jnp.int32, array.shape, 1) < array.shape[1] // 2
+
+
+def swapped(array):
+    half = array.shape[1] // 2
+    return jnp.concatenate([array[:, half:], array[:, :half]], axis=1)
+
+
+def fold_kernel(mask_ref, array_ref, folded_ref):
+    half = mask_ref.shape[1] // 2
+
+    @pl.loop(0, folded_ref.shape[1])
+    def _(pair):
+        tails = []
+        for member in range(2):
+            if len(array_ref.shape) == 5:
+                values = array_ref[member, 0, pair]
+            else:
+                values = array_ref[member, pair]
+            values = values * mask_ref[...]
+            first, second = values[:, :half], values[:, half:]
+            low = low_lanes(first)
+            turned = swapped(second)
+            kept = first + jnp.where(low, turned, jnp.zeros_like(turned))
+            folded_ref[0, pair, :, member * half : (member + 1) * half] = kept
+            tails.append(second if member == 0 else turned)
+        folded_ref[0, pair, :, 2 * half :] = jnp.where(low, tails[0], tails[1])
+
+
+def unfold_kernel(mask_ref, folded_ref, array_ref):
+    half = mask_ref.shape[1] // 2
+
+    @pl.loop(0, folded_ref.shape[1])
+    def _(pair):
+        tail = folded_ref[0, pair, :, 2 * half :]
+        low = low_lanes(tail)
+        for member in range(2):
+            kept = folded_ref[0, pair, :, member * half : (member + 1) * half]
+            own = tail if member == 0 else swapped(tail)
+            second = jnp.where(low, own, swapped(kept))
+            first = kept * mask_ref[:, :half]
+            second = second * mask_ref[:, half:]
+            if len(array_ref.shape) == 5:
+                array_ref[member, 0, pair, :, :half] = first
+                array_ref[member, 0, pair, :, half:] = second
+            else:
+                array_ref[member, pair, :, :half] = first
+                array_ref[member, pair, :, half:] = second
+
+
+def whole_spec(pairs, rows, columns, by_channel):
+    if by_channel:
+        return pl.BlockSpec((2, 1, pairs, rows, columns), lambda peer: (0, peer, 0, 0, 0))
+    return pl.BlockSpec((2, pairs, rows, columns), lambda peer: (0, 0, peer, 0))
+
+
+def mask_spec(rows, columns, by_channel):
+    if by_channel:
+        return pl.BlockSpec((rows, columns), lambda peer: (0, 0))
+    return pl.BlockSpec((rows, columns), lambda peer: (peer, 0))
+
+
+def fold(array, mask, by_channel):
+    width = lax.axis_size("row")
+    columns = array.shape[2]
+    if by_channel:
+        pairs, rows = array.shape[0] // (2 * width), array.shape[1]
+        array = array.reshape(2, width, pairs, rows, columns)
+    else:
+        pairs, rows = array.shape[0] // 2, array.shape[1] // width
+        array = array.reshape(2, pairs, width * rows, columns)
+    packed = 3 * (columns // 2)
+    return pl.pallas_call(
+        fold_kernel,
+        grid=(width,),
+        in_specs=[
+            mask_spec(rows, columns, by_channel),
+            whole_spec(pairs, rows, columns, by_channel),
+        ],
+        out_specs=pl.BlockSpec((1, pairs, rows, packed), lambda peer: (peer, 0, 0, 0)),
+        out_shape=jax.ShapeDtypeStruct((width, pairs, rows, packed), array.dtype),
+        cost_estimate=pl.CostEstimate(
+            flops=array.size * 4, bytes_accessed=array.size * 4, transcendentals=0
+        ),
+    )(mask, array)
+
+
+def unfold(moved, mask, by_channel):
+    width, pairs, rows, packed = moved.shape
+    columns = 2 * (packed // 3)
+    if by_channel:
+        shape = (2, width, pairs, rows, columns)
+    else:
+        shape = (2, pairs, width * rows, columns)
+    array = pl.pallas_call(
+        unfold_kernel,
+        grid=(width,),
+        in_specs=[
+            mask_spec(rows, columns, by_channel),
+            pl.BlockSpec((1, pairs, rows, packed), lambda peer: (peer, 0, 0, 0)),
+        ],
+        out_specs=whole_spec(pairs, rows, columns, by_channel),
+        out_shape=jax.ShapeDtypeStruct(shape, moved.dtype),
+        cost_estimate=pl.CostEstimate(
+            flops=moved.size * 4, bytes_accessed=moved.size * 4, transcendentals=0
+        ),
+    )(mask, moved)
+    if by_channel:
+        return array.reshape(2 * width * pairs, rows, columns)
+    return array.reshape(2 * pairs, width * rows, columns)
+
+
+def exchanged(array):
+    return lax.all_to_all(array, "row", split_axis=0, concat_axis=0, tiled=True)
+
+
+def to_channels(array, row_mask, full_mask):
+    return unfold(exchanged(fold(array, row_mask, True)), full_mask, False)
+
+
+def to_rows(array, row_mask, full_mask):
+    return unfold(exchanged(fold(array, full_mask, False)), row_mask, True)
+
+
+def reduced(sums):
+    weights_in, weights_out, norm_in, norm_out = sums
+    norms = jnp.concatenate([norm_in, norm_out], axis=0)
+    columns = weights_out.shape[1]
+    norms = jnp.pad(norms, ((0, columns - norms.shape[0]), (0, 0))).T
+    flat = jnp.concatenate([weights_in, weights_out, norms], axis=1).astype(jnp.bfloat16)
+    width = lax.axis_size("row")
+    parts = flat.reshape(width, flat.shape[0] // width, flat.shape[1])
+    parts = lax.all_to_all(parts, "row", split_axis=0, concat_axis=0, tiled=True)
+    summed = jnp.sum(parts.astype(jnp.float32), axis=0).astype(jnp.bfloat16)
+    copies = jnp.broadcast_to(summed[None], (width,) + summed.shape)
+    total = exchanged(copies).reshape(flat.shape).astype(jnp.float32)
+    split = weights_in.shape[1]
+    norms = total[:, split + columns : split + columns + 4].T
+    return (total[:, :split], total[:, split : split + columns], norms[:2], norms[2:])
 
 
 def layer_inputs(pair_rows, pair_mask, weight_inner, gain_inner, bias_inner, hidden):
@@ -140,6 +283,10 @@
     row_crop = lax.dynamic_slice_in_dim(crop_mask, row_start, row_count)
     same_chain = row_chain[:, None] == chain_ids[None, :]
     pair_mask = jnp.where(same_chain, row_crop[:, None] * crop_mask[None, :], 0).astype(jnp.float32)
+    row_mask = pair_mask.astype(jnp.bfloat16)
+    full_mask = jnp.where(
+        chain_ids[:, None] == chain_ids[None, :], crop_mask[:, None] * crop_mask[None, :], 0
+    ).astype(jnp.bfloat16)
     pair_rows = pair_in[0]
     grad_top = upstream[0]
 
@@ -152,16 +299,10 @@
             bias_in[0, direction],
             hidden,
         )
-        left_channels, right_channels = (
-            lax.all_to_all(left_edges, "row", split_axis=0, concat_axis=1, tiled=True),
-            lax.all_to_all(right_edges, "row", split_axis=0, concat_axis=1, tiled=True),
-        )
-        product = lax.all_to_all(
-            triangle_forward(left_channels, right_channels, outgoing),
-            "row",
-            split_axis=1,
-            concat_axis=0,
-            tiled=True,
+        left_channels = to_channels(left_edges, row_mask, full_mask)
+        right_channels = to_channels(right_edges, row_mask, full_mask)
+        product = to_rows(
+            triangle_forward(left_channels, right_channels, outgoing), row_mask, full_mask
         )
         updated, saved_out = layer_output(
             source,
@@ -178,14 +319,12 @@
         grad_product, grad_gate, grad_weight_out, grad_norm_out = output_backward(
             grad_pair, saved_in[6], saved_out, gain_out[0, direction], weight_out[0, direction]
         )
-        grad_channels = lax.all_to_all(grad_product, "row", split_axis=0, concat_axis=1, tiled=True)
+        grad_channels = to_channels(grad_product, row_mask, full_mask)
         left_grads, right_grads = triangle_backward(
             grad_channels, left_channels, right_channels, outgoing
         )
-        grad_leftside, grad_rightside = (
-            lax.all_to_all(left_grads, "row", split_axis=1, concat_axis=0, tiled=True),
-            lax.all_to_all(right_grads, "row", split_axis=1, concat_axis=0, tiled=True),
-        )
+        grad_leftside = to_rows(left_grads, row_mask, full_mask)
+        grad_rightside = to_rows(right_grads, row_mask, full_mask)
         branch_grad, grad_weight_in, grad_norm_in = input_backward(
             grad_leftside,
             grad_rightside,
@@ -208,13 +347,11 @@
         jnp.bfloat16
     )
     passed_back = passed_along(grad_input, "section", -1)
-    stacked = [jnp.stack([sums_outgoing[member], sums_incoming[member]]) for member in range(4)]
-    totals = (
-        lax.psum(stacked[0].astype(jnp.bfloat16), "row").astype(jnp.float32),
-        lax.psum(stacked[1].astype(jnp.bfloat16), "row").astype(jnp.float32),
-        lax.psum(stacked[2].astype(jnp.bfloat16), "row").astype(jnp.float32),
-        lax.psum(stacked[3].astype(jnp.bfloat16), "row").astype(jnp.float32),
-    )
+    incoming_totals = reduced(sums_incoming)
+    outgoing_totals = reduced(sums_outgoing)
+    totals = [
+        jnp.stack([outgoing_totals[member], incoming_totals[member]]) for member in range(4)
+    ]
     inverse_n = 1.0 / pair_rows.shape[1]
     return (
         passed_back[None],

time: 916 us -> 842 us (0.919)
  Pallas kernels: 0 us -> 191 us
  waiting for transfers between devices: 432 us -> 278 us
  blocking collectives: 125 us -> 41 us
  local copies, waits for them, and re-layouts: 138 us -> 69.1 us
  starting transfers between devices: 47.3 us -> 71 us
  other arithmetic: 81.4 us -> 99.1 us
  between operations: 15.4 us -> 1.86 us
  matrix products: 67.3 us -> 79.4 us
    pallas_call x0 -> x24, Pallas kernels: none -> 191 us  [the longest x12 95.9 us: unfold(): pl.pallas_call(unfold_kernel, grid=(width,), in_specs=[mask_spec(rows, co...]
    all_to_all x10 -> x15, waiting for transfers between devices: 383 us -> 273 us  [the longest x13 270 us: exchanged(): return lax.all_to_all(array, 'row', split_axis=0, concat_axis=0, tiled=True)]
    all_to_all x2 -> x1, blocking collectives: 105 us -> 41 us  [exchanged(): return lax.all_to_all(array, 'row', split_axis=0, concat_axis=0, tiled=True)]
    psum x1 -> x0, waiting for transfers between devices: 49 us -> none  [per_device(): lax.psum(stacked[0].astype(jnp.bfloat16), 'row').astype(jnp.float32)]
    convert_element_type x12 -> x0, local copies, waits for them, and re-layouts: 33.3 us -> none  [the longest x4 17.7 us: layer_output(): values = product.astype(jnp.float32)]
    all_to_all x10 -> x15, starting transfers between devices: 47.3 us -> 70.1 us  [the longest x13 61.4 us: exchanged(): return lax.all_to_all(array, 'row', split_axis=0, concat_axis=0, tiled=True)]
    psum x1 -> x0, blocking collectives: 20.7 us -> none  [per_device(): lax.psum(stacked[2].astype(jnp.bfloat16), 'row').astype(jnp.float32)]
    all_to_all x10 -> x0, local copies, waits for them, and re-layouts: 18.4 us -> none  [the longest x2 4.98 us: forward_update(): lax.all_to_all(right_edges, 'row', split_axis=0, concat_axis=1, tiled=True)]
  transfers between devices with their start and end apart: 12 -> 16, of which waited for: 11 -> 14; matrix products, arithmetic and copies ran while one was open for 11% -> 13% of each run, Pallas kernels for 0% -> 11%
where the time goes in v2:
time: 842 us; the launch traced here: 830 us
  waiting for transfers between devices  278 us (33%)
  Pallas kernels  191 us (23%)
  other arithmetic  99.1 us (12%)
  matrix products  79.4 us (9%)
  starting transfers between devices  71 us (8%)
  local copies, waits for them, and re-layouts  69.1 us (8%)
  blocking collectives  41 us (5%)
    all_to_all x13, waiting for transfers between devices, exchanged(): return lax.all_to_all(array, 'row', split_axis=0, concat_axis=0, tiled=True)  270 us
    pallas_call x12, Pallas kernels, unfold(): pl.pallas_call(unfold_kernel, grid=(width,), in_specs=[mask_spec(rows, co...  95.9 us
    pallas_call x12, Pallas kernels, fold(): pl.pallas_call(fold_kernel, grid=(width,), in_specs=[mask_spec(rows, colu...  94.9 us
    dot_general x24, matrix products, multiply(): jnp.einsum(pattern, first_part, second, preferred_element_type=jnp.float32)  79.4 us
    all_to_all x13, starting transfers between devices, exchanged(): return lax.all_to_all(array, 'row', split_axis=0, concat_axis=0, tiled=True)  61.4 us
    all_to_all x1, blocking collectives, exchanged(): return lax.all_to_all(array, 'row', split_axis=0, concat_axis=0, tiled=True)  41 us
    another operation x2, other arithmetic  19.9 us
    unnamed x70, local copies, waits for them, and re-layouts  19.6 us
  transfers between devices with their start and end apart: 16, of which 14 were waited for; matrix products, arithmetic and copies ran while one was open for 13% of the time, Pallas kernels for 11%

profile of v2, /device:TPU:0, one launch (start us, length us, event | category | flops | bytes accessed | tf_op | source)
XLA Modules:
  0.0 830.3 jit_solution(1527498237362479436)
XLA Ops:
  11.0 5.4 multiply_convert_fusion.12
  22.6 7.9 shard_map.139
  30.5 7.3 all-to-all-start.1
  42.2 7.9 shard_map.137
  50.1 24.7 %all-to-all-done.1.folded_ref = bf16[8,8,32,384]{3,2,1,0:T(8,128)(2,1)} async-done(((bf16[8,8,32,384]{3,2,1,0:T(8,128)(2,1)}), bf16[8,8,32,384]{3,2,1,0:T(8,128)(2,1)}, u32[]{:S(2)}, u32[]{:S(2)}) %all-to-all-start.1) | async-done | bytes 1572896 | tf_op jit(solution)/shard_map/all_to_all | solution.py:133
  79.9 8.0 shard_map.140
  88.0 27.8 %all-to-all-done.folded_ref = bf16[8,8,32,384]{3,2,1,0:T(8,128)(2,1)} async-done(((bf16[8,8,32,384]{3,2,1,0:T(8,128)(2,1)}), bf16[8,8,32,384]{3,2,1,0:T(8,128)(2,1)}, u32[]{:S(2)}, u32[]{:S(2)}) %all-to-all-start) | async-done | bytes 1572896 | tf_op jit(solution)/shard_map/all_to_all | solution.py:133
  115.8 8.0 shard_map.138
  128.1 8.0 shard_map.141
  140.8 36.4 %all-to-all-done.2.folded_ref = bf16[8,8,32,384]{3,2,1,0:T(8,128)(2,1)} async-done(((bf16[8,8,32,384]{3,2,1,0:T(8,128)(2,1)}), bf16[8,8,32,384]{3,2,1,0:T(8,128)(2,1)}, u32[]{:S(2)}, u32[]{:S(2)}) %all-to-all-start.2) | async-done | bytes 1572896 | tf_op jit(solution)/shard_map/all_to_all | solution.py:133
  177.2 7.9 shard_map.142
  199.6 5.4 multiply_convert_fusion.11
  211.2 7.9 shard_map.143
  228.0 7.9 shard_map.145
  235.9 24.2 %all-to-all-done.3.folded_ref = bf16[8,8,32,384]{3,2,1,0:T(8,128)(2,1)} async-done(((bf16[8,8,32,384]{3,2,1,0:T(8,128)(2,1)}), bf16[8,8,32,384]{3,2,1,0:T(8,128)(2,1)}, u32[]{:S(2)}, u32[]{:S(2)}) %all-to-all-start.3) | async-done | bytes 1572896 | tf_op jit(solution)/shard_map/all_to_all | solution.py:133
  264.4 8.1 shard_map.144
  272.4 28.5 %all-to-all-done.4.folded_ref = bf16[8,8,32,384]{3,2,1,0:T(8,128)(2,1)} async-done(((bf16[8,8,32,384]{3,2,1,0:T(8,128)(2,1)}), bf16[8,8,32,384]{3,2,1,0:T(8,128)(2,1)}, u32[]{:S(2)}, u32[]{:S(2)}) %all-to-all-start.4) | async-done | bytes 1572896 | tf_op jit(solution)/shard_map/all_to_all | solution.py:133
  301.0 8.0 shard_map.146
  313.3 8.0 shard_map.147
  335.3 27.2 %all-to-all-done.5.folded_ref = bf16[8,8,32,384]{3,2,1,0:T(8,128)(2,1)} async-done(((bf16[8,8,32,384]{3,2,1,0:T(8,128)(2,1)}), bf16[8,8,32,384]{3,2,1,0:T(8,128)(2,1)}, u32[]{:S(2)}, u32[]{:S(2)}) %all-to-all-start.5) | async-done | bytes 1572896 | tf_op jit(solution)/shard_map/all_to_all | solution.py:133
  362.6 7.9 shard_map.148
  387.4 7.9 shard_map.149
  395.3 41.0 %all_to_all.80.folded_ref = bf16[8,8,32,384]{3,2,1,0:T(8,128)(2,1)} all-to-all(bf16[8,8,32,384]{3,2,1,0:T(8,128)(2,1)} %shard_map.149), channel_id=1, replica_groups=mesh['section'=4,'row'=8] {'row'}, dimensions={0} | all-to-all | bytes 3145728 | tf_op jit(solution)/shard_map/all_to_all | solution.py:133
  436.2 8.1 shard_map.150
  448.6 7.9 shard_map.153
  465.3 7.9 shard_map.151
  473.3 23.9 %all-to-all-done.8.folded_ref = bf16[8,8,32,384]{3,2,1,0:T(8,128)(2,1)} async-done(((bf16[8,8,32,384]{3,2,1,0:T(8,128)(2,1)}), bf16[8,8,32,384]{3,2,1,0:T(8,128)(2,1)}, u32[]{:S(2)}, u32[]{:S(2)}) %all-to-all-start.8) | async-done | bytes 1572896 | tf_op jit(solution)/shard_map/all_to_all | solution.py:133
  519.5 7.9 shard_map.154
  531.6 5.3 copy.141
  538.0 7.9 shard_map.152
  550.0 5.3 copy.140
  555.3 10.0 %multiply_convert_fusion.8 = (bf16[128,32,256]{0,2,1:T(8,128)(2,1)S(1)}, bf16[128,32,256]{0,2,1:T(8,128)(2,1)S(1)}, bf16[128,32,256]{0,2,1:T(8,128)(2,1)S(1)}, bf16[128,32,256]{0,2,1:T(8,128)(2,1)S(1)}) fusion(f32[512,32,256]{0,2,1:T(8,128)} %copy-done.1, f32[128,32,256]{0,2,1:T(8,128)} %copy.140, f32[32,256]{1,0:T(8,128)S(1)} %get-tuple-element.66, ...), kind=kLoop, calls=%fused_computation.94 | loop fusion | flops 23068672 | bytes 33587200 | tf_op jit(solution)/shard_map/convert.49
  578.8 8.6 %fusion.35 = (bf16[32,256,128]{1,2,0:T(8,128)(2,1)}, bf16[32,256,128]{1,2,0:T(8,128)(2,1)S(1)}) fusion(f32[32,256,128]{1,2,0:T(8,128)} %get-tuple-element.78, f32[32,256,128]{1,2,0:T(8,128)} %copy-done.19, f32[32,256]{1,0:T(8,128)S(1)} %broadcast_multiply_fusion.4, f32[32,256]{1,0:T(8,128)S(1)} %broadcast_multiply_fusion.9, ...), kind=kLoop, calls=%fused_computation.49 | loop fusion | flops 17825792 | bytes 21103104 | tf_op jit(solution)/shard_map/convert_element_type | solution.py:212
  599.2 7.8 shard_map.155
  607.0 6.0 all-to-all-start.9
  613.0 35.7 %all-to-all-done.9.folded_ref = bf16[8,8,32,384]{3,2,1,0:T(8,128)(2,1)} async-done(((bf16[8,8,32,384]{3,2,1,0:T(8,128)(2,1)}), bf16[8,8,32,384]{3,2,1,0:T(8,128)(2,1)}, u32[]{:S(2)}, u32[]{:S(2)}) %all-to-all-start.9) | async-done | bytes 1572896 | tf_op jit(solution)/shard_map/all_to_all | solution.py:133
  652.9 8.1 shard_map.156
  665.3 7.9 shard_map.159
  673.3 5.9 all-to-all-start.11
  683.5 7.9 shard_map.157
  691.4 24.5 %all-to-all-done.11.folded_ref = bf16[8,8,32,384]{3,2,1,0:T(8,128)(2,1)} async-done(((bf16[8,8,32,384]{3,2,1,0:T(8,128)(2,1)}), bf16[8,8,32,384]{3,2,1,0:T(8,128)(2,1)}, u32[]{:S(2)}, u32[]{:S(2)}) %all-to-all-start.11) | async-done | bytes 1572896 | tf_op jit(solution)/shard_map/all_to_all | solution.py:133
  732.3 8.0 shard_map.160
  744.3 5.3 copy.153
  749.6 7.6 all-to-all-done.10.folded_ref
  757.2 7.9 shard_map.158
  769.1 5.3 copy.151
  774.4 10.0 %multiply_convert_fusion.3 = (bf16[128,32,256]{0,2,1:T(8,128)(2,1)S(1)}, bf16[128,32,256]{0,2,1:T(8,128)(2,1)S(1)}, bf16[128,32,256]{0,2,1:T(8,128)(2,1)S(1)}, bf16[128,32,256]{0,2,1:T(8,128)(2,1)S(1)}) fusion(f32[512,32,256]{0,2,1:T(8,128)} %copy-done, f32[128,32,256]{0,2,1:T(8,128)} %copy.151, f32[32,256]{1,0:T(8,128)S(1)} %get-tuple-element.66, ...), kind=kLoop, calls=%fused_computation.87 | loop fusion | flops 23068672 | bytes 33587200 | tf_op jit(solution)/shard_map/convert.45
  809.5 8.0 all-to-all-done.13
  (195 shorter events, 248.3 us)
Async XLA Ops:
  3.3 188.6 %copy-start.24 = (bf16[1,1,128,640]{2,3,1,0:T(8,128)(2,1)}, bf16[1,1,128,640]{2,3,1,0:T(8,128)(2,1)S(1)}, u32[]{:S(2)}) copy-start(bf16[1,1,128,640]{2,3,1,0:T(8,128)(2,1)S(1)} %copy.210) | copy-start | bytes 491524
  3.3 4.5 copy-start.29
  3.4 4.5 copy-start.30
  3.4 4.5 copy-start.27
  3.4 4.5 copy-start.28
  11.0 7.0 copy-start
  30.5 44.4 %all-to-all-start.1 = ((bf16[8,8,32,384]{3,2,1,0:T(8,128)(2,1)}), bf16[8,8,32,384]{3,2,1,0:T(8,128)(2,1)}, u32[]{:S(2)}, u32[]{:S(2)}) async-start(bf16[8,8,32,384]{3,2,1,0:T(8,128)(2,1)} %shard_map.139), calls=%async_computation.1 | async-start | bytes 3145728 | tf_op jit(solution)/shard_map/all_to_all | solution.py:133
  74.8 40.9 %all-to-all-start = ((bf16[8,8,32,384]{3,2,1,0:T(8,128)(2,1)}), bf16[8,8,32,384]{3,2,1,0:T(8,128)(2,1)}, u32[]{:S(2)}, u32[]{:S(2)}) async-start(bf16[8,8,32,384]{3,2,1,0:T(8,128)(2,1)} %shard_map.137), calls=%async_computation | async-start | bytes 3145728 | tf_op jit(solution)/shard_map/all_to_all | solution.py:133
  128.1 12.5 %copy-start.31 = (f32[1,2,128]{2,1,0:T(2,128)S(1)}, f32[1,2,128]{2,1,0:T(2,128)}, u32[]{:S(2)}) copy-start(f32[1,2,128]{2,1,0:T(2,128)} %param.18) | copy-start | bytes 3076
  128.1 12.5 %copy-start.32 = (f32[1,2,128]{2,1,0:T(2,128)S(1)}, f32[1,2,128]{2,1,0:T(2,128)}, u32[]{:S(2)}) copy-start(f32[1,2,128]{2,1,0:T(2,128)} %param.19) | copy-start | bytes 3076
  136.1 41.1 %all-to-all-start.2 = ((bf16[8,8,32,384]{3,2,1,0:T(8,128)(2,1)}), bf16[8,8,32,384]{3,2,1,0:T(8,128)(2,1)}, u32[]{:S(2)}, u32[]{:S(2)}) async-start(bf16[8,8,32,384]{3,2,1,0:T(8,128)(2,1)} %shard_map.141), calls=%async_computation.2 | async-start | bytes 3145728 | tf_op jit(solution)/shard_map/all_to_all | solution.py:133
  185.2 4.3 copy-start.4
  185.2 5.1 copy-start.26
  192.0 3.8 copy-start.19
  195.8 1.3 copy-start.13
  199.6 7.0 copy-start.1
  219.1 40.9 %all-to-all-start.3 = ((bf16[8,8,32,384]{3,2,1,0:T(8,128)(2,1)}), bf16[8,8,32,384]{3,2,1,0:T(8,128)(2,1)}, u32[]{:S(2)}, u32[]{:S(2)}) async-start(bf16[8,8,32,384]{3,2,1,0:T(8,128)(2,1)} %shard_map.143), calls=%async_computation.3 | async-start | bytes 3145728 | tf_op jit(solution)/shard_map/all_to_all | solution.py:133
  260.1 40.9 %all-to-all-start.4 = ((bf16[8,8,32,384]{3,2,1,0:T(8,128)(2,1)}), bf16[8,8,32,384]{3,2,1,0:T(8,128)(2,1)}, u32[]{:S(2)}, u32[]{:S(2)}) async-start(bf16[8,8,32,384]{3,2,1,0:T(8,128)(2,1)} %shard_map.145), calls=%async_computation.4 | async-start | bytes 3145728 | tf_op jit(solution)/shard_map/all_to_all | solution.py:133
  321.2 41.3 %all-to-all-start.5 = ((bf16[8,8,32,384]{3,2,1,0:T(8,128)(2,1)}), bf16[8,8,32,384]{3,2,1,0:T(8,128)(2,1)}, u32[]{:S(2)}, u32[]{:S(2)}) async-start(bf16[8,8,32,384]{3,2,1,0:T(8,128)(2,1)} %shard_map.147), calls=%async_computation.5 | async-start | bytes 3145728 | tf_op jit(solution)/shard_map/all_to_all | solution.py:133
  370.5 4.5 copy-start.5
  372.6 2.9 copy-start.2
  372.6 3.5 copy-start.7
  381.2 3.7 copy-start.10
  456.5 40.6 %all-to-all-start.8 = ((bf16[8,8,32,384]{3,2,1,0:T(8,128)(2,1)}), bf16[8,8,32,384]{3,2,1,0:T(8,128)(2,1)}, u32[]{:S(2)}, u32[]{:S(2)}) async-start(bf16[8,8,32,384]{3,2,1,0:T(8,128)(2,1)} %shard_map.153), calls=%async_computation.8 | async-start | bytes 3145728 | tf_op jit(solution)/shard_map/all_to_all | solution.py:133
  497.2 40.8 %all-to-all-start.7 = ((bf16[8,8,32,384]{3,2,1,0:T(8,128)(2,1)}), bf16[8,8,32,384]{3,2,1,0:T(8,128)(2,1)}, u32[]{:S(2)}, u32[]{:S(2)}) async-start(bf16[8,8,32,384]{3,2,1,0:T(8,128)(2,1)} %shard_map.151), calls=%async_computation.7 | async-start | bytes 3145728 | tf_op jit(solution)/shard_map/all_to_all | solution.py:133
  508.1 2.5 copy-start.3
  510.7 4.4 copy-start.14
  515.1 1.3 copy-start.20
  515.1 2.9 copy-start.8
  515.1 3.6 copy-start.23
  555.3 10.0 %copy-start.15 = (bf16[32,256,128]{1,2,0:T(8,128)(2,1)S(1)}, bf16[32,256,128]{1,2,0:T(8,128)(2,1)}, u32[]{:S(2)}) copy-start(bf16[32,256,128]{1,2,0:T(8,128)(2,1)} %copy-done.13) | copy-start | bytes 6291460
  566.6 2.8 copy-start.21
  573.7 33.3 %all-to-all-start.14 = ((bf16[8,16,896]{2,1,0:T(8,128)(2,1)}), bf16[8,16,896]{2,1,0:T(8,128)(2,1)S(1)}, u32[]{:S(2)}, u32[]{:S(2)}) async-start(bf16[8,16,896]{2,1,0:T(8,128)(2,1)} %pad_maximum_fusion.11), calls=%async_computation.14 | async-start | bytes 458752 | tf_op jit(solution)/shard_map/all_to_all | solution.py:152
  578.8 8.6 %copy-start.6 = (f32[128,32,256]{2,1,0:T(8,128)S(1)}, f32[128,32,256]{2,1,0:T(8,128)}, u32[]{:S(2)}) copy-start(f32[128,32,256]{2,1,0:T(8,128)} %convert.172) | copy-start | bytes 12582916
  578.8 8.9 %copy-start.11 = (f32[32,256,128]{1,2,0:T(8,128)S(1)}, f32[32,256,128]{1,2,0:T(8,128)}, u32[]{:S(2)}) copy-start(f32[32,256,128]{1,2,0:T(8,128)} %get-tuple-element.78) | copy-start | bytes 12582916
  587.4 5.5 copy-start.16
  592.9 3.7 copy-start.9
  607.0 41.8 %all-to-all-start.9 = ((bf16[8,8,32,384]{3,2,1,0:T(8,128)(2,1)}), bf16[8,8,32,384]{3,2,1,0:T(8,128)(2,1)}, u32[]{:S(2)}, u32[]{:S(2)}) async-start(bf16[8,8,32,384]{3,2,1,0:T(8,128)(2,1)} %shard_map.155), calls=%async_computation.9 | async-start | bytes 3145728 | tf_op jit(solution)/shard_map/all_to_all | solution.py:133
  649.5 23.8 %all-to-all-start.15 = ((bf16[8,16,896]{2,1,0:T(8,128)(2,1)}), bf16[8,16,896]{2,1,0:T(8,128)(2,1)S(1)}, u32[]{:S(2)}, u32[]{:S(2)}) async-start(bf16[8,16,896]{2,1,0:T(8,128)(2,1)} %broadcast_in_dim.18), calls=%async_computation.15 | async-start | bytes 458752 | tf_op jit(solution)/shard_map/all_to_all | solution.py:133
  673.3 42.7 %all-to-all-start.11 = ((bf16[8,8,32,384]{3,2,1,0:T(8,128)(2,1)}), bf16[8,8,32,384]{3,2,1,0:T(8,128)(2,1)}, u32[]{:S(2)}, u32[]{:S(2)}) async-start(bf16[8,8,32,384]{3,2,1,0:T(8,128)(2,1)} %shard_map.159), calls=%async_computation.11 | async-start | bytes 3145728 | tf_op jit(solution)/shard_map/all_to_all | solution.py:133
  716.0 41.2 %all-to-all-start.10 = ((bf16[8,8,32,384]{3,2,1,0:T(8,128)(2,1)}), bf16[8,8,32,384]{3,2,1,0:T(8,128)(2,1)}, u32[]{:S(2)}, u32[]{:S(2)}) async-start(bf16[8,8,32,384]{3,2,1,0:T(8,128)(2,1)} %shard_map.157), calls=%async_computation.10 | async-start | bytes 3145728 | tf_op jit(solution)/shard_map/all_to_all | solution.py:133
  725.4 3.4 copy-start.12
  774.4 10.0 %copy-start.22 = (bf16[32,256,128]{1,2,0:T(8,128)(2,1)S(1)}, bf16[32,256,128]{1,2,0:T(8,128)(2,1)}, u32[]{:S(2)}) copy-start(bf16[32,256,128]{1,2,0:T(8,128)(2,1)} %fusion.24) | copy-start | bytes 6291460
  785.7 2.9 copy-start.18
  793.0 12.2 %all-to-all-start.12 = ((bf16[8,16,896]{2,1,0:T(8,128)(2,1)}), bf16[8,16,896]{2,1,0:T(8,128)(2,1)S(1)}, u32[]{:S(2)}, u32[]{:S(2)}) async-start(bf16[8,16,896]{2,1,0:T(8,128)(2,1)} %pad_maximum_fusion.10), calls=%async_computation.12 | async-start | bytes 458752 | tf_op jit(solution)/shard_map/all_to_all | solution.py:152
  796.7 3.9 copy-start.17
  801.3 24.4 %collective-permute-start = (bf16[32,256,128]{1,2,0:T(8,128)(2,1)S(1)}, bf16[32,256,128]{1,2,0:T(8,128)(2,1)}, u32[]{:S(2)}, u32[]{:S(2)}) collective-permute-start(bf16[32,256,128]{1,2,0:T(8,128)(2,1)S(1)} %fusion.36), channel_id=1, source_target_pairs={{0,24},{8,0},{16,8},{24,16},{1,25},{9,1},{17,9},{25,17},{2,26},{10... | collective-permute-start | bytes 6291464 | tf_op jit(solution)/shard_map/ppermute | solution.py:12
  806.0 11.5 %all-to-all-start.13 = ((bf16[8,16,896]{2,1,0:T(8,128)(2,1)}), bf16[8,16,896]{2,1,0:T(8,128)(2,1)S(1)}, u32[]{:S(2)}, u32[]{:S(2)}) async-start(bf16[8,16,896]{2,1,0:T(8,128)(2,1)} %broadcast_in_dim.17), calls=%async_computation.13 | async-start | bytes 458752 | tf_op jit(solution)/shard_map/all_to_all | solution.py:133
  (1 other events, 1.3 us)

commit v3 on v2

--- a/solution.py
+++ b/solution.py
@@ -1,7 +1,10 @@
+import functools
+
 import jax
 import jax.numpy as jnp
 from jax import lax
 from jax.experimental import pallas as pl
+from jax.experimental.pallas import tpu as pltpu
 from jax.sharding import PartitionSpec as P
 
 epsilon = 1e-05
@@ -28,15 +31,10 @@
 def fold_kernel(mask_ref, array_ref, folded_ref):
     half = mask_ref.shape[1] // 2
 
-    @pl.loop(0, folded_ref.shape[1])
-    def _(pair):
+    for pair in range(folded_ref.shape[1]):
         tails = []
         for member in range(2):
-            if len(array_ref.shape) == 5:
-                values = array_ref[member, 0, pair]
-            else:
-                values = array_ref[member, pair]
-            values = values * mask_ref[...]
+            values = array_ref[member, 0, pair] * mask_ref[...]
             first, second = values[:, :half], values[:, half:]
             low = low_lanes(first)
             turned = swapped(second)
@@ -49,8 +47,7 @@
 def unfold_kernel(mask_ref, folded_ref, array_ref):
     half = mask_ref.shape[1] // 2
 
-    @pl.loop(0, folded_ref.shape[1])
-    def _(pair):
+    for pair in range(folded_ref.shape[1]):
         tail = folded_ref[0, pair, :, 2 * half :]
         low = low_lanes(tail)
         for member in range(2):
@@ -59,86 +56,154 @@
             second = jnp.where(low, own, swapped(kept))
             first = kept * mask_ref[:, :half]
             second = second * mask_ref[:, half:]
-            if len(array_ref.shape) == 5:
-                array_ref[member, 0, pair, :, :half] = first
-                array_ref[member, 0, pair, :, half:] = second
-            else:
-                array_ref[member, pair, :, :half] = first
-                array_ref[member, pair, :, half:] = second
-
-
-def whole_spec(pairs, rows, columns, by_channel):
-    if by_channel:
-        return pl.BlockSpec((2, 1, pairs, rows, columns), lambda peer: (0, peer, 0, 0, 0))
-    return pl.BlockSpec((2, pairs, rows, columns), lambda peer: (0, 0, peer, 0))
-
-
-def mask_spec(rows, columns, by_channel):
-    if by_channel:
-        return pl.BlockSpec((rows, columns), lambda peer: (0, 0))
-    return pl.BlockSpec((rows, columns), lambda peer: (peer, 0))
-
-
-def fold(array, mask, by_channel):
+            array_ref[member, 0, pair, :, :half] = first
+            array_ref[member, 0, pair, :, half:] = second
+
+
+def fold(array, mask):
     width = lax.axis_size("row")
-    columns = array.shape[2]
-    if by_channel:
-        pairs, rows = array.shape[0] // (2 * width), array.shape[1]
-        array = array.reshape(2, width, pairs, rows, columns)
-    else:
-        pairs, rows = array.shape[0] // 2, array.shape[1] // width
-        array = array.reshape(2, pairs, width * rows, columns)
+    pairs, rows, columns = array.shape[0] // (2 * width), array.shape[1], array.shape[2]
     packed = 3 * (columns // 2)
     return pl.pallas_call(
         fold_kernel,
         grid=(width,),
         in_specs=[
-            mask_spec(rows, columns, by_channel),
-            whole_spec(pairs, rows, columns, by_channel),
+            pl.BlockSpec((rows, columns), lambda peer: (0, 0)),
+            pl.BlockSpec((2, 1, pairs, rows, columns), lambda peer: (0, peer, 0, 0, 0)),
         ],
         out_specs=pl.BlockSpec((1, pairs, rows, packed), lambda peer: (peer, 0, 0, 0)),
         out_shape=jax.ShapeDtypeStruct((width, pairs, rows, packed), array.dtype),
         cost_estimate=pl.CostEstimate(
             flops=array.size * 4, bytes_accessed=array.size * 4, transcendentals=0
         ),
-    )(mask, array)
-
-
-def unfold(moved, mask, by_channel):
+    )(mask, array.reshape(2, width, pairs, rows, columns))
+
+
+def unfold(moved, mask):
     width, pairs, rows, packed = moved.shape
     columns = 2 * (packed // 3)
-    if by_channel:
-        shape = (2, width, pairs, rows, columns)
-    else:
-        shape = (2, pairs, width * rows, columns)
     array = pl.pallas_call(
         unfold_kernel,
         grid=(width,),
         in_specs=[
-            mask_spec(rows, columns, by_channel),
+            pl.BlockSpec((rows, columns), lambda peer: (0, 0)),
             pl.BlockSpec((1, pairs, rows, packed), lambda peer: (peer, 0, 0, 0)),
         ],
-        out_specs=whole_spec(pairs, rows, columns, by_channel),
-        out_shape=jax.ShapeDtypeStruct(shape, moved.dtype),
+        out_specs=pl.BlockSpec((2, 1, pairs, rows, columns), lambda peer: (0, peer, 0, 0, 0)),
+        out_shape=jax.ShapeDtypeStruct((2, width, pairs, rows, columns), moved.dtype),
         cost_estimate=pl.CostEstimate(
             flops=moved.size * 4, bytes_accessed=moved.size * 4, transcendentals=0
         ),
     )(mask, moved)
-    if by_channel:
-        return array.reshape(2 * width * pairs, rows, columns)
-    return array.reshape(2 * pairs, width * rows, columns)
+    return array.reshape(2 * width * pairs, rows, columns)
 
 
 def exchanged(array):
     return lax.all_to_all(array, "row", split_axis=0, concat_axis=0, tiled=True)
 
 
-def to_channels(array, row_mask, full_mask):
-    return unfold(exchanged(fold(array, row_mask, True)), full_mask, False)
-
-
-def to_rows(array, row_mask, full_mask):
-    return unfold(exchanged(fold(array, full_mask, False)), row_mask, True)
+def to_channels(array, row_mask):
+    return exchanged(fold(array, row_mask))
+
+
+def to_rows(folded, row_mask):
+    return unfold(exchanged(folded), row_mask)
+
+
+def read_pair(ref):
+    peers, _, rows, packed = ref.shape
+    folded = ref[:, 0]
+    if rows % 16:
+        folded = folded.astype(jnp.float32)
+    return folded.reshape(peers * rows, packed).astype(jnp.bfloat16)
+
+
+def write_pair(ref, members, mask):
+    peers, _, rows, packed = ref.shape
+    half = packed // 3
+    kept, tails = [], []
+    for member, values in enumerate(members):
+        values = values.astype(jnp.bfloat16) * mask
+        first, second = values[:, :half], values[:, half:]
+        low = low_lanes(first)
+        turned = swapped(second)
+        kept.append(first + jnp.where(low, turned, jnp.zeros_like(turned)))
+        tails.append(second if member == 0 else turned)
+    folded = jnp.concatenate(kept + [jnp.where(low, tails[0], tails[1])], axis=1)
+    if rows % 16:
+        folded = folded.astype(jnp.float32)
+    ref[:, 0] = folded.reshape(peers, rows, packed).astype(jnp.bfloat16)
+
+
+def member_of(folded, member, mask):
+    half = folded.shape[1] // 3
+    tail = folded[:, 2 * half :]
+    kept = folded[:, member * half : (member + 1) * half]
+    own = tail if member == 0 else swapped(tail)
+    second = jnp.where(low_lanes(tail), own, swapped(kept))
+    return jnp.concatenate([kept, second], axis=1) * mask
+
+
+def contracted(first, second, first_axis, second_axis):
+    return lax.dot_general(
+        first,
+        second,
+        (((first_axis,), (second_axis,)), ((), ())),
+        preferred_element_type=jnp.float32,
+    )
+
+
+def forward_kernel(outgoing, mask_ref, left_ref, right_ref, product_ref):
+    mask = mask_ref[...]
+    left_pair, right_pair = read_pair(left_ref), read_pair(right_ref)
+    members = []
+    for member in range(2):
+        left_edges = member_of(left_pair, member, mask)
+        right_edges = member_of(right_pair, member, mask)
+        axis = 1 if outgoing else 0
+        members.append(contracted(left_edges, right_edges, axis, axis))
+    write_pair(product_ref, members, mask)
+
+
+def backward_kernel(
+    outgoing, mask_ref, grad_ref, left_ref, right_ref, left_grad_ref, right_grad_ref
+):
+    mask = mask_ref[...]
+    grad_pair = read_pair(grad_ref)
+    left_pair, right_pair = read_pair(left_ref), read_pair(right_ref)
+    left_grads, right_grads = [], []
+    for member in range(2):
+        grad = member_of(grad_pair, member, mask)
+        left_edges = member_of(left_pair, member, mask)
+        right_edges = member_of(right_pair, member, mask)
+        if outgoing:
+            left_grads.append(contracted(grad, right_edges, 1, 0))
+            right_grads.append(contracted(grad, left_edges, 0, 0))
+        else:
+            left_grads.append(contracted(right_edges, grad, 1, 1))
+            right_grads.append(contracted(left_edges, grad, 1, 0))
+    write_pair(left_grad_ref, left_grads, mask)
+    write_pair(right_grad_ref, right_grads, mask)
+
+
+def triangle(kernel, outgoing, outputs, mask, *operands):
+    peers, pairs, rows, packed = operands[0].shape
+    block = pl.BlockSpec((peers, 1, rows, packed), lambda pair: (0, pair, 0, 0))
+    shape = jax.ShapeDtypeStruct(operands[0].shape, operands[0].dtype)
+    residues = mask.shape[0]
+    return pl.pallas_call(
+        functools.partial(kernel, outgoing),
+        grid=(pairs,),
+        in_specs=[pl.BlockSpec(mask.shape, lambda pair: (0, 0))] + [block] * len(operands),
+        out_specs=[block] * outputs,
+        out_shape=[shape] * outputs,
+        cost_estimate=pl.CostEstimate(
+            flops=4 * outputs * pairs * residues**3,
+            bytes_accessed=2 * operands[0].size * (len(operands) + outputs),
+            transcendentals=0,
+        ),
+        compiler_params=pltpu.CompilerParams(vmem_limit_bytes=32 * 1024 * 1024),
+    )(mask, *operands)
 
 
 def reduced(sums):
@@ -172,24 +237,6 @@
     right_edges = (pair_mask * right_sigmoid * projected[3 * hidden :]).astype(jnp.bfloat16)
     saved_in = (normal_in, inverse_scale, normed, projected, left_sigmoid, right_sigmoid, gating)
     return (left_edges, right_edges, saved_in)
-
-
-def triangle_forward(left_edges, right_edges, outgoing):
-    if outgoing:
-        product = multiply("hik,hjk->hij", left_edges, right_edges)
-    else:
-        product = multiply("hki,hkj->hij", left_edges, right_edges)
-    return product.astype(jnp.bfloat16)
-
-
-def triangle_backward(grad_product, left_edges, right_edges, outgoing):
-    if outgoing:
-        grad_leftside = multiply("hij,hjk->hik", grad_product, right_edges)
-        grad_rightside = multiply("hij,hik->hjk", grad_product, left_edges)
-    else:
-        grad_leftside = multiply("hij,hkj->hki", grad_product, right_edges)
-        grad_rightside = multiply("hij,hki->hkj", grad_product, left_edges)
-    return (grad_leftside.astype(jnp.bfloat16), grad_rightside.astype(jnp.bfloat16))
 
 
 def layer_output(pair_rows, product, gating, gain_outer, bias_outer, weight_outer):
@@ -299,11 +346,12 @@
             bias_in[0, direction],
             hidden,
         )
-        left_channels = to_channels(left_edges, row_mask, full_mask)
-        right_channels = to_channels(right_edges, row_mask, full_mask)
-        product = to_rows(
-            triangle_forward(left_channels, right_channels, outgoing), row_mask, full_mask
-        )
+        left_channels = to_channels(left_edges, row_mask)
+        right_channels = to_channels(right_edges, row_mask)
+        (folded,) = triangle(
+            forward_kernel, outgoing, 1, full_mask, left_channels, right_channels
+        )
+        product = to_rows(folded, row_mask)
         updated, saved_out = layer_output(
             source,
             product,
@@ -319,12 +367,12 @@
         grad_product, grad_gate, grad_weight_out, grad_norm_out = output_backward(
             grad_pair, saved_in[6], saved_out, gain_out[0, direction], weight_out[0, direction]
         )
-        grad_channels = to_channels(grad_product, row_mask, full_mask)
-        left_grads, right_grads = triangle_backward(
-            grad_channels, left_channels, right_channels, outgoing
-        )
-        grad_leftside = to_rows(left_grads, row_mask, full_mask)
-        grad_rightside = to_rows(right_grads, row_mask, full_mask)
+        grad_channels = to_channels(grad_product, row_mask)
+        left_grads, right_grads = triangle(
+            backward_kernel, outgoing, 2, full_mask, grad_channels, left_channels, right_channels
+        )
+        grad_leftside = to_rows(left_grads, row_mask)
+        grad_rightside = to_rows(right_grads, row_mask)
         branch_grad, grad_weight_in, grad_norm_in = input_backward(
             grad_leftside,
             grad_rightside,

time: 842 us -> 776 us (0.922)
  blocking collectives: 41 us -> 165 us
  Pallas kernels: 191 us -> 94.6 us
  waiting for transfers between devices: 278 us -> 215 us
  matrix products: 79.4 us -> 55.9 us
  starting transfers between devices: 71 us -> 54.7 us
  local copies, waits for them, and re-layouts: 69.1 us -> 78.2 us
    all_to_all x1 -> x4, blocking collectives: 41 us -> 165 us  [exchanged(): return lax.all_to_all(array, 'row', split_axis=0, concat_axis=0, tiled=True)]
    pallas_call x24 -> x16, Pallas kernels: 191 us -> 94.6 us  [the longest x6 35.9 us: unfold(): pl.pallas_call(unfold_kernel, grid=(width,), in_specs=[pl.BlockSpec((rows...]
    all_to_all x13 -> x10, waiting for transfers between devices: 270 us -> 207 us  [exchanged(): return lax.all_to_all(array, 'row', split_axis=0, concat_axis=0, tiled=True)]
    dot_general x24 -> x18, matrix products: 79.4 us -> 55.9 us  [multiply(): jnp.einsum(pattern, first_part, second, preferred_element_type=jnp.float32)]
    all_to_all x13 -> x10, starting transfers between devices: 61.4 us -> 46.5 us  [exchanged(): return lax.all_to_all(array, 'row', split_axis=0, concat_axis=0, tiled=True)]
    unnamed x70 -> x144, local copies, waits for them, and re-layouts: 19.6 us -> 26.8 us
  transfers between devices with their start and end apart: 16 -> 13, of which waited for: 14 -> 11; matrix products, arithmetic and copies ran while one was open for 13% -> 13% of each run, Pallas kernels for 11% -> 5%
where the time goes in v3:
time: 776 us; the launch traced here: 766 us
  waiting for transfers between devices  215 us (28%)
  blocking collectives  165 us (21%)
  other arithmetic  101 us (13%)
  Pallas kernels  94.6 us (12%)
  local copies, waits for them, and re-layouts  78.2 us (10%)
  matrix products  55.9 us (7%)
  starting transfers between devices  54.7 us (7%)
    all_to_all x10, waiting for transfers between devices, exchanged(): return lax.all_to_all(array, 'row', split_axis=0, concat_axis=0, tiled=True)  207 us
    all_to_all x4, blocking collectives, exchanged(): return lax.all_to_all(array, 'row', split_axis=0, concat_axis=0, tiled=True)  165 us
    dot_general x18, matrix products, multiply(): jnp.einsum(pattern, first_part, second, preferred_element_type=jnp.float32)  55.9 us
    all_to_all x10, starting transfers between devices, exchanged(): return lax.all_to_all(array, 'row', split_axis=0, concat_axis=0, tiled=True)  46.5 us
    pallas_call x6, Pallas kernels, unfold(): pl.pallas_call(unfold_kernel, grid=(width,), in_specs=[pl.BlockSpec((rows...  35.9 us
    pallas_call x6, Pallas kernels, fold(): pl.pallas_call(fold_kernel, grid=(width,), in_specs=[pl.BlockSpec((rows,...  35.1 us
    unnamed x144, local copies, waits for them, and re-layouts  26.8 us
    pallas_call x4, Pallas kernels, triangle(): pl.pallas_call(functools.partial(kernel, outgoing), grid=(pairs,), in_spe...  23.7 us
  transfers between devices with their start and end apart: 13, of which 11 were waited for; matrix products, arithmetic and copies ran while one was open for 13% of the time, Pallas kernels for 5%

profile of v3, /device:TPU:0, one launch (start us, length us, event | category | flops | bytes accessed | tf_op | source)
XLA Modules:
  0.0 766.2 jit_solution(5973396113498010649)
XLA Ops:
  11.6 4.9 multiply_convert_fusion.12
  21.0 5.9 shard_map.138
  26.9 7.3 all-to-all-start.1
  34.2 4.6 copy.123
  38.8 5.8 shard_map.137
  44.6 26.5 %all-to-all-done.1.right_ref = bf16[8,8,32,384]{3,2,1,0:T(8,128)(2,1)S(1)} async-done(((bf16[8,8,32,384]{3,2,1,0:T(8,128)(2,1)}), bf16[8,8,32,384]{3,2,1,0:T(8,128)(2,1)S(1)}, u32[]{:S(2)}, u32[]{:S(2)}) %all-to-all-start.1) | async-done | bytes 1572896 | tf_op jit(solution)/shard_map/all_to_all | solution.py:102
  75.0 37.0 %all-to-all-done.left_ref = bf16[8,8,32,384]{3,2,1,0:T(8,128)(2,1)S(1)} async-done(((bf16[8,8,32,384]{3,2,1,0:T(8,128)(2,1)}), bf16[8,8,32,384]{3,2,1,0:T(8,128)(2,1)S(1)}, u32[]{:S(2)}, u32[]{:S(2)}) %all-to-all-start) | async-done | bytes 1572896 | tf_op jit(solution)/shard_map/all_to_all | solution.py:102
  123.6 34.6 %all-to-all-done.2.folded_ref = bf16[8,8,32,384]{3,2,1,0:T(8,128)(2,1)} async-done(((bf16[8,8,32,384]{3,2,1,0:T(8,128)(2,1)}), bf16[8,8,32,384]{3,2,1,0:T(8,128)(2,1)}, u32[]{:S(2)}, u32[]{:S(2)}) %all-to-all-start.2) | async-done | bytes 1572896 | tf_op jit(solution)/shard_map/all_to_all | solution.py:102
  158.2 6.0 shard_map.140
  171.1 4.7 convert_reduce_fusion
  179.8 5.3 multiply_convert_fusion.10
  186.7 4.6 copy.129
  191.3 5.8 shard_map.142
  201.5 4.6 copy.128
  206.0 5.8 shard_map.141
  211.9 26.2 %all-to-all-done.4.right_ref = bf16[8,8,32,384]{3,2,1,0:T(8,128)(2,1)} async-done(((bf16[8,8,32,384]{3,2,1,0:T(8,128)(2,1)}), bf16[8,8,32,384]{3,2,1,0:T(8,128)(2,1)}, u32[]{:S(2)}, u32[]{:S(2)}) %all-to-all-start.4) | async-done | bytes 1572896 | tf_op jit(solution)/shard_map/all_to_all | solution.py:102
  238.1 40.8 %all_to_all.80.left_ref = bf16[8,8,32,384]{3,2,1,0:T(8,128)(2,1)S(1)} all-to-all(bf16[8,8,32,384]{3,2,1,0:T(8,128)(2,1)} %shard_map.141), channel_id=1, replica_groups=mesh['section'=4,'row'=8] {'row'}, dimensions={0} | all-to-all | bytes 3145728 | tf_op jit(solution)/shard_map/all_to_all | solution.py:102
  278.8 6.3 shard_map.143
  287.5 4.7 all-to-all-start.5
  296.3 5.3 add_divide_fusion
  301.6 26.8 %all-to-all-done.5.folded_ref = bf16[8,8,32,384]{3,2,1,0:T(8,128)(2,1)} async-done(((bf16[8,8,32,384]{3,2,1,0:T(8,128)(2,1)}), bf16[8,8,32,384]{3,2,1,0:T(8,128)(2,1)}, u32[]{:S(2)}, u32[]{:S(2)}) %all-to-all-start.5) | async-done | bytes 1572896 | tf_op jit(solution)/shard_map/all_to_all | solution.py:102
  328.4 6.0 shard_map.144
  340.0 5.2 fusion.55
  351.4 5.8 shard_map.145
  357.2 40.6 %all_to_all.81.grad_ref = bf16[8,8,32,384]{3,2,1,0:T(8,128)(2,1)S(1)} all-to-all(bf16[8,8,32,384]{3,2,1,0:T(8,128)(2,1)} %shard_map.145), channel_id=1, replica_groups=mesh['section'=4,'row'=8] {'row'}, dimensions={0} | all-to-all | bytes 3145728 | tf_op jit(solution)/shard_map/all_to_all | solution.py:102
  399.3 6.5 shard_map.146
  405.8 40.4 %all_to_all.82.folded_ref = bf16[8,8,32,384]{3,2,1,0:T(8,128)(2,1)} all-to-all(bf16[8,8,32,384]{3,2,1,0:T(8,128)(2,1)S(1)} %get-tuple-element.9), channel_id=1, replica_groups=mesh['section'=4,'row'=8] {'row'}, dimensions={0} | all-to-all | bytes 3145728 | tf_op jit(solution)/shard_map/all_to_all | solution.py:102
  468.8 6.0 shard_map.147
  478.9 5.3 copy.135
  486.8 6.0 shard_map.148
  496.9 5.3 copy.136
  502.2 10.0 %multiply_convert_fusion.8 = (bf16[128,32,256]{0,2,1:T(8,128)(2,1)S(1)}, bf16[128,32,256]{0,2,1:T(8,128)(2,1)S(1)}, bf16[128,32,256]{0,2,1:T(8,128)(2,1)S(1)}, bf16[128,32,256]{0,2,1:T(8,128)(2,1)S(1)}) fusion(f32[512,32,256]{0,2,1:T(8,128)} %copy-done.8, f32[128,32,256]{0,2,1:T(8,128)} %copy.135, f32[32,256]{1,0:T(8,128)S(1)} %get-tuple-element.74, ...), kind=kLoop, calls=%fused_computation.94 | loop fusion | flops 23068672 | bytes 33587200 | tf_op jit(solution)/shard_map/convert.49
  528.2 8.5 %fusion.35 = (bf16[32,256,128]{1,2,0:T(8,128)(2,1)}, bf16[32,256,128]{1,2,0:T(8,128)(2,1)S(1)}) fusion(f32[32,256,128]{1,2,0:T(8,128)} %get-tuple-element.86, f32[32,256,128]{1,2,0:T(8,128)} %copy-done.29, f32[32,256]{1,0:T(8,128)S(1)} %broadcast_multiply_fusion.4, f32[32,256]{1,0:T(8,128)} %copy-done.40, bf16[32,256,128]{1,2,0:T(8,128)(2,1)} %copy-done.23, ...), kind=kLoop, calls=%fused_computation.49 | loop fusion | flops 17825792 | bytes 21103104 | tf_op jit(solution)/shard_map/convert_element_type | solution.py:259
  537.1 5.3 fusion.54
  548.6 5.8 shard_map.149
  554.5 6.0 all-to-all-start.9
  561.1 36.1 %all-to-all-done.9.grad_ref = bf16[8,8,32,384]{3,2,1,0:T(8,128)(2,1)} async-done(((bf16[8,8,32,384]{3,2,1,0:T(8,128)(2,1)}), bf16[8,8,32,384]{3,2,1,0:T(8,128)(2,1)}, u32[]{:S(2)}, u32[]{:S(2)}) %all-to-all-start.9) | async-done | bytes 1572896 | tf_op jit(solution)/shard_map/all_to_all | solution.py:102
  602.3 6.9 shard_map.150
  611.6 42.9 %all_to_all.83.folded_ref = bf16[8,8,32,384]{3,2,1,0:T(8,128)(2,1)} all-to-all(bf16[8,8,32,384]{3,2,1,0:T(8,128)(2,1)} %copy-done.6), channel_id=1, replica_groups=mesh['section'=4,'row'=8] {'row'}, dimensions={0} | all-to-all | bytes 3145728 | tf_op jit(solution)/shard_map/all_to_all | solution.py:102
  654.5 4.6 all-to-all-start.11
  670.7 6.0 shard_map.151
  680.8 5.3 copy.146
  686.1 9.0 %all-to-all-done.11.folded_ref = bf16[8,8,32,384]{3,2,1,0:T(8,128)(2,1)} async-done(((bf16[8,8,32,384]{3,2,1,0:T(8,128)(2,1)}), bf16[8,8,32,384]{3,2,1,0:T(8,128)(2,1)}, u32[]{:S(2)}, u32[]{:S(2)}) %all-to-all-start.11) | async-done | bytes 1572896 | tf_op jit(solution)/shard_map/all_to_all | solution.py:102
  695.2 6.0 shard_map.152
  705.2 5.3 copy.147
  710.6 10.0 %multiply_convert_fusion.3 = (bf16[128,32,256]{0,2,1:T(8,128)(2,1)S(1)}, bf16[128,32,256]{0,2,1:T(8,128)(2,1)S(1)}, bf16[128,32,256]{0,2,1:T(8,128)(2,1)S(1)}, bf16[128,32,256]{0,2,1:T(8,128)(2,1)S(1)}) fusion(f32[512,32,256]{0,2,1:T(8,128)} %copy-done.7, f32[128,32,256]{0,2,1:T(8,128)} %copy.146, f32[32,256]{1,0:T(8,128)S(1)} %copy-done.37, ...), kind=kLoop, calls=%fused_computation.87 | loop fusion | flops 23068672 | bytes 33587200 | tf_op jit(solution)/shard_map/convert.45
  745.5 8.0 %all-to-all-done.13 = bf16[8,16,896]{2,1,0:T(8,128)(2,1)S(1)} async-done(((bf16[8,16,896]{2,1,0:T(8,128)(2,1)}), bf16[8,16,896]{2,1,0:T(8,128)(2,1)S(1)}, u32[]{:S(2)}, u32[]{:S(2)}) %all-to-all-start.13) | async-done | bytes 229408 | tf_op jit(solution)/shard_map/all_to_all | solution.py:102
  756.6 5.1 collective-permute-done
  (252 shorter events, 182.5 us)
Async XLA Ops:
  3.2 293.1 %copy-start.41 = (bf16[128,640]{1,0:T(8,128)(2,1)}, bf16[128,640]{1,0:T(8,128)(2,1)S(1)}, u32[]{:S(2)}) copy-start(bf16[128,640]{1,0:T(8,128)(2,1)S(1)} %get-tuple-element.68) | copy-start | bytes 491524
  3.3 5.8 copy-start.43
  3.4 4.5 copy-start.66
  3.4 4.5 copy-start.67
  3.4 5.0 copy-start.54
  3.4 5.0 copy-start.55
  6.8 4.8 copy-start.9
  7.9 163.2 %copy-start.34 = (f32[32,256]{1,0:T(8,128)}, f32[32,256]{1,0:T(8,128)S(1)}, u32[]{:S(2)}) copy-start(f32[32,256]{1,0:T(8,128)S(1)} %add_rsqrt_fusion.3) | copy-start | bytes 98308
  9.1 493.1 %copy-start.36 = (f32[32,256]{1,0:T(8,128)}, f32[32,256]{1,0:T(8,128)S(1)}, u32[]{:S(2)}) copy-start(f32[32,256]{1,0:T(8,128)S(1)} %get-tuple-element.74) | copy-start | bytes 98308
  11.6 6.4 copy-start.7
  26.9 44.3 %all-to-all-start.1 = ((bf16[8,8,32,384]{3,2,1,0:T(8,128)(2,1)}), bf16[8,8,32,384]{3,2,1,0:T(8,128)(2,1)S(1)}, u32[]{:S(2)}, u32[]{:S(2)}) async-start(bf16[8,8,32,384]{3,2,1,0:T(8,128)(2,1)} %shard_map.138), calls=%async_computation.1 | async-start | bytes 3145728 | tf_op jit(solution)/shard_map/all_to_all | solution.py:102
  71.2 40.8 %all-to-all-start = ((bf16[8,8,32,384]{3,2,1,0:T(8,128)(2,1)}), bf16[8,8,32,384]{3,2,1,0:T(8,128)(2,1)S(1)}, u32[]{:S(2)}, u32[]{:S(2)}) async-start(bf16[8,8,32,384]{3,2,1,0:T(8,128)(2,1)} %shard_map.137), calls=%async_computation | async-start | bytes 3145728 | tf_op jit(solution)/shard_map/all_to_all | solution.py:102
  74.8 46.8 %copy-start.68 = (f32[1,2,128]{2,1,0:T(2,128)S(1)}, f32[1,2,128]{2,1,0:T(2,128)}, u32[]{:S(2)}) copy-start(f32[1,2,128]{2,1,0:T(2,128)} %param.18) | copy-start | bytes 3076
  75.0 46.6 %copy-start.69 = (f32[1,2,128]{2,1,0:T(2,128)S(1)}, f32[1,2,128]{2,1,0:T(2,128)}, u32[]{:S(2)}) copy-start(f32[1,2,128]{2,1,0:T(2,128)} %param.19) | copy-start | bytes 3076
  117.0 41.1 %all-to-all-start.2 = ((bf16[8,8,32,384]{3,2,1,0:T(8,128)(2,1)}), bf16[8,8,32,384]{3,2,1,0:T(8,128)(2,1)}, u32[]{:S(2)}, u32[]{:S(2)}) async-start(bf16[8,8,32,384]{3,2,1,0:T(8,128)(2,1)} %copy-done.2), calls=%async_computation.2 | async-start | bytes 3145728 | tf_op jit(solution)/shard_map/all_to_all | solution.py:102
  164.1 5.2 copy-start.49
  171.1 4.7 copy-start.29
  171.1 6.1 copy-start.56
  171.1 6.1 copy-start.63
  175.8 341.2 %copy-start.40 = (f32[32,256]{1,0:T(8,128)}, f32[32,256]{1,0:T(8,128)S(1)}, u32[]{:S(2)}) copy-start(f32[32,256]{1,0:T(8,128)S(1)} %broadcast_multiply_fusion.9) | copy-start | bytes 98308
  179.7 7.0 copy-start.8
  197.1 40.9 %all-to-all-start.4 = ((bf16[8,8,32,384]{3,2,1,0:T(8,128)(2,1)}), bf16[8,8,32,384]{3,2,1,0:T(8,128)(2,1)}, u32[]{:S(2)}, u32[]{:S(2)}) async-start(bf16[8,8,32,384]{3,2,1,0:T(8,128)(2,1)} %shard_map.142), calls=%async_computation.4 | async-start | bytes 3145728 | tf_op jit(solution)/shard_map/all_to_all | solution.py:102
  287.5 40.9 %all-to-all-start.5 = ((bf16[8,8,32,384]{3,2,1,0:T(8,128)(2,1)}), bf16[8,8,32,384]{3,2,1,0:T(8,128)(2,1)}, u32[]{:S(2)}, u32[]{:S(2)}) async-start(bf16[8,8,32,384]{3,2,1,0:T(8,128)(2,1)} %copy-done.3), calls=%async_computation.5 | async-start | bytes 3145728 | tf_op jit(solution)/shard_map/all_to_all | solution.py:102
  334.4 4.5 copy-start.15
  405.8 40.4 %copy-start.5 = (bf16[8,8,32,384]{3,2,1,0:T(8,128)(2,1)}, bf16[8,8,32,384]{3,2,1,0:T(8,128)(2,1)S(1)}, u32[]{:S(2)}) copy-start(bf16[8,8,32,384]{3,2,1,0:T(8,128)(2,1)S(1)} %get-tuple-element.10) | copy-start | bytes 4718596
  405.8 44.9 %copy-start.65 = (f32[128]{0:T(128)S(1)}, f32[128]{0:T(128)}, u32[]{:S(2)}) copy-start(f32[128]{0:T(128)} %get-tuple-element.42) | copy-start | bytes 1540
  405.8 44.9 %copy-start.64 = (f32[128]{0:T(128)S(1)}, f32[128]{0:T(128)}, u32[]{:S(2)}) copy-start(f32[128]{0:T(128)} %get-tuple-element.93) | copy-start | bytes 1540
  446.2 40.6 %all-to-all-start.8 = ((bf16[8,8,32,384]{3,2,1,0:T(8,128)(2,1)}), bf16[8,8,32,384]{3,2,1,0:T(8,128)(2,1)}, u32[]{:S(2)}, u32[]{:S(2)}) async-start(bf16[8,8,32,384]{3,2,1,0:T(8,128)(2,1)} %copy-done.5), calls=%async_computation.8 | async-start | bytes 3145728 | tf_op jit(solution)/shard_map/all_to_all | solution.py:102
  502.2 10.0 %copy-start.25 = (bf16[32,256,128]{1,2,0:T(8,128)(2,1)S(1)}, bf16[32,256,128]{1,2,0:T(8,128)(2,1)}, u32[]{:S(2)}) copy-start(bf16[32,256,128]{1,2,0:T(8,128)(2,1)} %copy-done.23) | copy-start | bytes 6291460
  522.8 31.6 %all-to-all-start.14 = ((bf16[8,16,896]{2,1,0:T(8,128)(2,1)}), bf16[8,16,896]{2,1,0:T(8,128)(2,1)S(1)}, u32[]{:S(2)}, u32[]{:S(2)}) async-start(bf16[8,16,896]{2,1,0:T(8,128)(2,1)} %pad_maximum_fusion.11), calls=%async_computation.14 | async-start | bytes 458752 | tf_op jit(solution)/shard_map/all_to_all | solution.py:217
  528.1 8.6 %copy-start.16 = (f32[128,32,256]{2,1,0:T(8,128)S(1)}, f32[128,32,256]{2,1,0:T(8,128)}, u32[]{:S(2)}) copy-start(f32[128,32,256]{2,1,0:T(8,128)} %convert.172) | copy-start | bytes 12582916
  528.1 8.9 %copy-start.21 = (f32[32,256,128]{1,2,0:T(8,128)S(1)}, f32[32,256,128]{1,2,0:T(8,128)}, u32[]{:S(2)}) copy-start(f32[32,256,128]{1,2,0:T(8,128)} %get-tuple-element.86) | copy-start | bytes 12582916
  528.1 8.9 %copy-start.39 = (f32[32,256]{1,0:T(8,128)S(1)}, f32[32,256]{1,0:T(8,128)}, u32[]{:S(2)}) copy-start(f32[32,256]{1,0:T(8,128)} %copy-done.38) | copy-start | bytes 98308
  528.1 8.9 %copy-start.46 = (f32[32,256]{1,0:T(8,128)S(1)}, f32[32,256]{1,0:T(8,128)}, u32[]{:S(2)}) copy-start(f32[32,256]{1,0:T(8,128)} %copy-done.45) | copy-start | bytes 98308
  528.2 8.9 %copy-start.51 = (bf16[1,2,128,128]{3,2,1,0:T(8,128)(2,1)S(1)}, bf16[1,2,128,128]{3,2,1,0:T(8,128)(2,1)}, u32[]{:S(2)}) copy-start(bf16[1,2,128,128]{3,2,1,0:T(8,128)(2,1)} %param.15) | copy-start | bytes 196612
  528.2 8.9 %copy-start.57 = (f32[128]{0:T(128)S(1)}, f32[128]{0:T(128)}, u32[]{:S(2)}) copy-start(f32[128]{0:T(128)} %get-tuple-element.80) | copy-start | bytes 1540
  528.2 8.9 %copy-start.61 = (f32[128]{0:T(128)S(1)}, f32[128]{0:T(128)}, u32[]{:S(2)}) copy-start(f32[128]{0:T(128)} %get-tuple-element.96) | copy-start | bytes 1540
  536.7 5.6 copy-start.26
  554.5 42.7 %all-to-all-start.9 = ((bf16[8,8,32,384]{3,2,1,0:T(8,128)(2,1)}), bf16[8,8,32,384]{3,2,1,0:T(8,128)(2,1)}, u32[]{:S(2)}, u32[]{:S(2)}) async-start(bf16[8,8,32,384]{3,2,1,0:T(8,128)(2,1)} %shard_map.149), calls=%async_computation.9 | async-start | bytes 3145728 | tf_op jit(solution)/shard_map/all_to_all | solution.py:102
  598.6 12.9 %all-to-all-start.15 = ((bf16[8,16,896]{2,1,0:T(8,128)(2,1)}), bf16[8,16,896]{2,1,0:T(8,128)(2,1)S(1)}, u32[]{:S(2)}, u32[]{:S(2)}) async-start(bf16[8,16,896]{2,1,0:T(8,128)(2,1)} %broadcast_in_dim.18), calls=%async_computation.15 | async-start | bytes 458752 | tf_op jit(solution)/shard_map/all_to_all | solution.py:102
  611.5 47.5 %copy-start.11 = (bf16[1,32,256,128]{2,3,1,0:T(8,128)(2,1)S(1)}, bf16[1,32,256,128]{2,3,1,0:T(8,128)(2,1)}, u32[]{:S(2)}) copy-start(bf16[1,32,256,128]{2,3,1,0:T(8,128)(2,1)} %copy-done.9) | copy-start | bytes 6291460
  611.5 47.5 %copy-start.35 = (f32[32,256]{1,0:T(8,128)S(1)}, f32[32,256]{1,0:T(8,128)}, u32[]{:S(2)}) copy-start(f32[32,256]{1,0:T(8,128)} %copy-done.34) | copy-start | bytes 98308
  654.5 40.7 %all-to-all-start.11 = ((bf16[8,8,32,384]{3,2,1,0:T(8,128)(2,1)}), bf16[8,8,32,384]{3,2,1,0:T(8,128)(2,1)}, u32[]{:S(2)}, u32[]{:S(2)}) async-start(bf16[8,8,32,384]{3,2,1,0:T(8,128)(2,1)} %copy-done.4), calls=%async_computation.11 | async-start | bytes 3145728 | tf_op jit(solution)/shard_map/all_to_all | solution.py:102
  705.2 5.4 copy-start.37
  710.6 10.0 %copy-start.32 = (bf16[32,256,128]{1,2,0:T(8,128)(2,1)S(1)}, bf16[32,256,128]{1,2,0:T(8,128)(2,1)}, u32[]{:S(2)}) copy-start(bf16[32,256,128]{1,2,0:T(8,128)(2,1)} %fusion.24) | copy-start | bytes 6291460
  729.2 12.1 %all-to-all-start.12 = ((bf16[8,16,896]{2,1,0:T(8,128)(2,1)}), bf16[8,16,896]{2,1,0:T(8,128)(2,1)S(1)}, u32[]{:S(2)}, u32[]{:S(2)}) async-start(bf16[8,16,896]{2,1,0:T(8,128)(2,1)} %pad_maximum_fusion.10), calls=%async_computation.12 | async-start | bytes 458752 | tf_op jit(solution)/shard_map/all_to_all | solution.py:217
  737.3 24.4 %collective-permute-start = (bf16[32,256,128]{1,2,0:T(8,128)(2,1)S(1)}, bf16[32,256,128]{1,2,0:T(8,128)(2,1)}, u32[]{:S(2)}, u32[]{:S(2)}) collective-permute-start(bf16[32,256,128]{1,2,0:T(8,128)(2,1)S(1)} %fusion.36), channel_id=1, source_target_pairs={{0,24},{8,0},{16,8},{24,16},{1,25},{9,1},{17,9},{25,17},{2,26},{10... | collective-permute-start | bytes 6291464 | tf_op jit(solution)/shard_map/ppermute | solution.py:15
  742.0 11.5 %all-to-all-start.13 = ((bf16[8,16,896]{2,1,0:T(8,128)(2,1)}), bf16[8,16,896]{2,1,0:T(8,128)(2,1)S(1)}, u32[]{:S(2)}, u32[]{:S(2)}) async-start(bf16[8,16,896]{2,1,0:T(8,128)(2,1)} %broadcast_in_dim.17), calls=%async_computation.13 | async-start | bytes 458752 | tf_op jit(solution)/shard_map/all_to_all | solution.py:102
  (35 other events, 88.8 us)
